TPU v7x, 512 devices: a whole 4x8x8 slice. The times are simulated.
512 devices in a mesh: seq: 64 (over z, y), head: 8 (over x, core).
Axes of the slice: x: 4, y: 8, z: 8, core: 2. Of those that a mesh axis runs over, the one named last changes fastest.
Arguments:
- queries: bfloat16 [32768, 4096], P('seq', 'head'), may hold values from -1.796875 to 1.796875
- keys: bfloat16 [32768, 4096], P('seq', 'head'), may hold values from -1.796875 to 1.796875
- values: bfloat16 [32768, 4096], P('seq', 'head'), may hold values from -40 to 40
- out_grad: bfloat16 [32768, 4096], P('seq', 'head'), may hold values from -6 to 6
- gain: float32 [4096], P('head'), may hold values from 0.1 to 1.9
- doc_starts: int32 [25], replicated, may hold values from 0 to 32512, as said below
Outputs:
- query_grad: bfloat16 [32768, 4096], P('seq', 'head')
- key_grad: bfloat16 [32768, 4096], P('seq', 'head')
- value_grad: bfloat16 [32768, 4096], P('seq', 'head')
Inputs may be any that keep to these rules, and one draw needn't show every extreme that they name: `doc_starts`: sorted and distinct; the first is 0; every multiple of 8192 is among them; one of the first three quarters of the pack is a single document of 8192 tokens, each of the other quarters holds 8 documents; the last document starts at 32512.
All inputs are finite; a program needn't handle non-finite values.
Results may differ from a plain program's by a relative error of at most 0.0058.
Values sent between devices are 32-bit elements; how exact they have to be, the bound alone decides.
No kernel may reach another device: no remote copies, remote signals or barrier semaphores. Data moves between devices by JAX's collectives and lax.ppermute only.
A program may use at most 128 MiB of HBM per device.

v0:
```python
import jax
import jax.numpy as jnp
from jax import lax
from jax.sharding import PartitionSpec as P

DH = 128
WIDTH = 4096


EPSILON = 1e-06


def shifted(value, axis, steps):
    count = lax.axis_size(axis)
    first, last = (max(0, -steps), min(count, count - steps))
    return lax.ppermute(value, axis, [(source, source + steps) for source in range(first, last)])


def doc_of(doc_starts, positions):
    started = (doc_starts[None, :] <= positions[:, None]).astype(jnp.int32)
    return jnp.sum(started, axis=1) - 1


def on_device(queries, keys, values, out_grad, gain, doc_starts):
    rows_here = queries.shape[0]
    head_count = queries.shape[1] // DH
    device_pos = lax.axis_index("seq")
    first_pos = device_pos * rows_here
    within = jnp.arange(rows_here, dtype=jnp.int32)
    doc_ids = doc_of(doc_starts, first_pos + within)
    edge_docs = doc_of(doc_starts, jnp.stack([first_pos - 1, first_pos + rows_here]))
    before_doc = edge_docs[0]
    after_doc = edge_docs[1]
    query_heads = queries.reshape(rows_here, head_count, DH)
    key_heads = keys.reshape(rows_here, head_count, DH)
    value_heads = values.reshape(rows_here, head_count, DH)
    allowed = (within[None, :] <= within[:, None]) & (doc_ids[:, None] == doc_ids[None, :])
    scores = jnp.einsum("thd,shd->hts", query_heads, key_heads, preferred_element_type=jnp.float32)
    masked_scores = jnp.where(allowed[None], scores, 0.0).astype(jnp.bfloat16)
    chosen = (doc_ids == after_doc).astype(jnp.bfloat16)
    kv_state = jnp.einsum(
        "shd,she->hde",
        key_heads * chosen[:, None, None],
        value_heads,
        preferred_element_type=jnp.float32,
    )
    opens_next = after_doc != doc_ids[0]
    seq_count = lax.axis_size("seq")
    steps_back = seq_count // 4 - 1
    empty_state = jnp.zeros_like(kv_state)

    def forward_step(turn_index, carried_in):
        joined = jnp.where(opens_next, kv_state, carried_in + kv_state)
        return shifted(joined, "seq", 1)

    prefix = lax.fori_loop(0, steps_back, forward_step, empty_state)
    prefix_bf = prefix.astype(jnp.bfloat16)
    head_from = (doc_ids == doc_ids[0]).astype(jnp.float32)[:, None, None]
    intra_part = jnp.einsum(
        "hts,she->the", masked_scores, value_heads, preferred_element_type=jnp.float32
    )
    carried = jnp.einsum("thd,hde->the", query_heads, prefix_bf, preferred_element_type=jnp.float32)
    attended = intra_part + head_from * carried
    gain_heads = gain.reshape(head_count, DH)
    scaled = gain_heads * out_grad.reshape(rows_here, head_count, DH).astype(jnp.float32)
    totals = lax.psum(
        (jnp.sum(attended * attended, axis=(1, 2)), jnp.sum(attended * scaled, axis=(1, 2))), "head"
    )
    inverse = lax.rsqrt(totals[0] / WIDTH + EPSILON)[:, None, None]
    normed_grad = (
        scaled * inverse
        - attended * (inverse * inverse * inverse) * (totals[1][:, None, None] / WIDTH)
    ).astype(jnp.bfloat16)
    picked = (doc_ids == before_doc).astype(jnp.bfloat16)
    grad_state = jnp.einsum(
        "thd,the->hde",
        query_heads * picked[:, None, None],
        normed_grad,
        preferred_element_type=jnp.float32,
    )
    opens_here = doc_ids[rows_here - 1] != before_doc

    def backward_step(turn_index, carried_in):
        joined = jnp.where(opens_here, grad_state, carried_in + grad_state)
        return shifted(joined, "seq", -1)

    later_state = lax.fori_loop(0, steps_back, backward_step, empty_state)
    later_bf = later_state.astype(jnp.bfloat16)
    products = jnp.einsum(
        "the,she->hts", normed_grad, value_heads, preferred_element_type=jnp.float32
    )
    masked_products = jnp.where(allowed[None], products, 0.0).astype(jnp.bfloat16)
    tail_to = (doc_ids == doc_ids[rows_here - 1]).astype(jnp.float32)[:, None, None]
    query_grad = jnp.einsum(
        "hts,shd->thd", masked_products, key_heads, preferred_element_type=jnp.float32
    ) + head_from * jnp.einsum(
        "the,hde->thd", normed_grad, prefix_bf, preferred_element_type=jnp.float32
    )
    key_grad = jnp.einsum(
        "hts,thd->shd", masked_products, query_heads, preferred_element_type=jnp.float32
    ) + tail_to * jnp.einsum(
        "she,hde->shd", value_heads, later_bf, preferred_element_type=jnp.float32
    )
    value_grad = jnp.einsum(
        "hts,the->she", masked_scores, normed_grad, preferred_element_type=jnp.float32
    ) + tail_to * jnp.einsum(
        "shd,hde->she", key_heads, later_bf, preferred_element_type=jnp.float32
    )
    width_here = head_count * DH
    return (
        query_grad.astype(jnp.bfloat16).reshape(rows_here, width_here),
        key_grad.astype(jnp.bfloat16).reshape(rows_here, width_here),
        value_grad.astype(jnp.bfloat16).reshape(rows_here, width_here),
    )


def solution(mesh):
    placed = (
        P("seq", "head"),
        P("seq", "head"),
        P("seq", "head"),
        P("seq", "head"),
        P("head"),
        P(),
    )
    return jax.shard_map(
        on_device,
        mesh=mesh,
        in_specs=placed,
        out_specs=(P("seq", "head"), P("seq", "head"), P("seq", "head")),
        check_vma=False,
    )
```

profile of v0, /device:TPU:248, one launch (start us, length us, event | category | flops | bytes accessed | tf_op | source)
XLA Modules:
  0.0 409.6 jit_solution(8563980112028114105)
XLA Ops:
  9.1 181.5 %while.20 = (s32[]{:T(128)}, f32[4,128,128]{2,1,0:T(8,128)S(1)}, pred[]{:T(512)}, f32[4,128,128]{2,1,0:T(8,128)S(1)}, s32[]{:T(128)}) while((s32[]{:T(128)}, f32[4,128,128]{2,1,0:T(8,128)S(1)}, pred[]{:T(512)}, f32[4,128,128]{2,1,0:T(8,128)S(1)}, s32[]{:T(128)}) %tuple.46), condition=%wide.region_3.4_spmd, body=%wide.region_2.3_spmd.sunk | while | flops 131074 | bytes 1835110 | solution.py:56
  19.5 7.7 %collective-permute-start = (f32[4,128,128]{2,1,0:T(8,128)S(1)}, f32[4,128,128]{2,1,0:T(8,128)S(1)}, u32[]{:S(2)}, u32[]{:S(2)}) collective-permute-start(f32[4,128,128]{2,1,0:T(8,128)S(1)} %add_select_fusion.4), channel_id=1, source_target_pairs={{0,8},{8,16},{16,24},{24,32},{32,40},{40,48},{48,56},{56,64},{64,7... | collective-permute-start | bytes 786440 | tf_op jit(solution)/shard_map/while/body/eval_jaxpr/ppermute | solution.py:16
  32.0 7.7 %collective-permute-start = (f32[4,128,128]{2,1,0:T(8,128)S(1)}, f32[4,128,128]{2,1,0:T(8,128)S(1)}, u32[]{:S(2)}, u32[]{:S(2)}) collective-permute-start(f32[4,128,128]{2,1,0:T(8,128)S(1)} %add_select_fusion.4), channel_id=1, source_target_pairs={{0,8},{8,16},{16,24},{24,32},{32,40},{40,48},{48,56},{56,64},{64,7... | collective-permute-start | bytes 786440 | tf_op jit(solution)/shard_map/while/body/eval_jaxpr/ppermute | solution.py:16
  43.6 7.7 %collective-permute-start = (f32[4,128,128]{2,1,0:T(8,128)S(1)}, f32[4,128,128]{2,1,0:T(8,128)S(1)}, u32[]{:S(2)}, u32[]{:S(2)}) collective-permute-start(f32[4,128,128]{2,1,0:T(8,128)S(1)} %add_select_fusion.4), channel_id=1, source_target_pairs={{0,8},{8,16},{16,24},{24,32},{32,40},{40,48},{48,56},{56,64},{64,7... | collective-permute-start | bytes 786440 | tf_op jit(solution)/shard_map/while/body/eval_jaxpr/ppermute | solution.py:16
  55.2 7.7 %collective-permute-start = (f32[4,128,128]{2,1,0:T(8,128)S(1)}, f32[4,128,128]{2,1,0:T(8,128)S(1)}, u32[]{:S(2)}, u32[]{:S(2)}) collective-permute-start(f32[4,128,128]{2,1,0:T(8,128)S(1)} %add_select_fusion.4), channel_id=1, source_target_pairs={{0,8},{8,16},{16,24},{24,32},{32,40},{40,48},{48,56},{56,64},{64,7... | collective-permute-start | bytes 786440 | tf_op jit(solution)/shard_map/while/body/eval_jaxpr/ppermute | solution.py:16
  66.8 7.7 %collective-permute-start = (f32[4,128,128]{2,1,0:T(8,128)S(1)}, f32[4,128,128]{2,1,0:T(8,128)S(1)}, u32[]{:S(2)}, u32[]{:S(2)}) collective-permute-start(f32[4,128,128]{2,1,0:T(8,128)S(1)} %add_select_fusion.4), channel_id=1, source_target_pairs={{0,8},{8,16},{16,24},{24,32},{32,40},{40,48},{48,56},{56,64},{64,7... | collective-permute-start | bytes 786440 | tf_op jit(solution)/shard_map/while/body/eval_jaxpr/ppermute | solution.py:16
  78.4 7.7 %collective-permute-start = (f32[4,128,128]{2,1,0:T(8,128)S(1)}, f32[4,128,128]{2,1,0:T(8,128)S(1)}, u32[]{:S(2)}, u32[]{:S(2)}) collective-permute-start(f32[4,128,128]{2,1,0:T(8,128)S(1)} %add_select_fusion.4), channel_id=1, source_target_pairs={{0,8},{8,16},{16,24},{24,32},{32,40},{40,48},{48,56},{56,64},{64,7... | collective-permute-start | bytes 786440 | tf_op jit(solution)/shard_map/while/body/eval_jaxpr/ppermute | solution.py:16
  196.8 12.4 %all-reduce = (f32[512]{0:T(512)S(1)}, f32[512]{0:T(512)S(1)}) all-reduce(f32[512]{0:T(512)S(1)} %get-tuple-element.56, f32[512]{0:T(512)S(1)} %get-tuple-element.55), channel_id=1, replica_groups=mesh['seq'=64,'head'=8] {'head'}, use_global_device_ids=true, to_apply=%region_7.8 | all-reduce | flops 1024 | bytes 8192 | tf_op jit(solution)/shard_map/psum | solution.py:66
  213.5 186.0 %while.21 = (s32[]{:T(128)}, f32[4,128,128]{2,1,0:T(8,128)S(1)}, pred[]{:T(512)}, f32[4,128,128]{2,1,0:T(8,128)S(1)}, s32[]{:T(128)}) while((s32[]{:T(128)}, f32[4,128,128]{2,1,0:T(8,128)S(1)}, pred[]{:T(512)}, f32[4,128,128]{2,1,0:T(8,128)S(1)}, s32[]{:T(128)}) %tuple.49), condition=%wide.region_9.10_spmd, body=%wide.region_8.9_spmd.sunk | while | flops 131074 | bytes 1835110 | solution.py:87
  215.6 12.1 %collective-permute-done.1 = f32[4,128,128]{2,1,0:T(8,128)S(1)} collective-permute-done((f32[4,128,128]{2,1,0:T(8,128)S(1)}, f32[4,128,128]{2,1,0:T(8,128)S(1)}, u32[]{:S(2)}, u32[]{:S(2)}) %collective-permute-start.1) | collective-permute-done | bytes 262176 | tf_op jit(solution)/shard_map/while/body/eval_jaxpr/ppermute | solution.py:16
  229.7 10.8 %collective-permute-done.1 = f32[4,128,128]{2,1,0:T(8,128)S(1)} collective-permute-done((f32[4,128,128]{2,1,0:T(8,128)S(1)}, f32[4,128,128]{2,1,0:T(8,128)S(1)}, u32[]{:S(2)}, u32[]{:S(2)}) %collective-permute-start.1) | collective-permute-done | bytes 262176 | tf_op jit(solution)/shard_map/while/body/eval_jaxpr/ppermute | solution.py:16
  242.4 9.9 %collective-permute-done.1 = f32[4,128,128]{2,1,0:T(8,128)S(1)} collective-permute-done((f32[4,128,128]{2,1,0:T(8,128)S(1)}, f32[4,128,128]{2,1,0:T(8,128)S(1)}, u32[]{:S(2)}, u32[]{:S(2)}) %collective-permute-start.1) | collective-permute-done | bytes 262176 | tf_op jit(solution)/shard_map/while/body/eval_jaxpr/ppermute | solution.py:16
  254.3 9.7 %collective-permute-done.1 = f32[4,128,128]{2,1,0:T(8,128)S(1)} collective-permute-done((f32[4,128,128]{2,1,0:T(8,128)S(1)}, f32[4,128,128]{2,1,0:T(8,128)S(1)}, u32[]{:S(2)}, u32[]{:S(2)}) %collective-permute-start.1) | collective-permute-done | bytes 262176 | tf_op jit(solution)/shard_map/while/body/eval_jaxpr/ppermute | solution.py:16
  265.9 9.7 %collective-permute-done.1 = f32[4,128,128]{2,1,0:T(8,128)S(1)} collective-permute-done((f32[4,128,128]{2,1,0:T(8,128)S(1)}, f32[4,128,128]{2,1,0:T(8,128)S(1)}, u32[]{:S(2)}, u32[]{:S(2)}) %collective-permute-start.1) | collective-permute-done | bytes 262176 | tf_op jit(solution)/shard_map/while/body/eval_jaxpr/ppermute | solution.py:16
  277.5 9.7 %collective-permute-done.1 = f32[4,128,128]{2,1,0:T(8,128)S(1)} collective-permute-done((f32[4,128,128]{2,1,0:T(8,128)S(1)}, f32[4,128,128]{2,1,0:T(8,128)S(1)}, u32[]{:S(2)}, u32[]{:S(2)}) %collective-permute-start.1) | collective-permute-done | bytes 262176 | tf_op jit(solution)/shard_map/while/body/eval_jaxpr/ppermute | solution.py:16
  289.1 9.7 %collective-permute-done.1 = f32[4,128,128]{2,1,0:T(8,128)S(1)} collective-permute-done((f32[4,128,128]{2,1,0:T(8,128)S(1)}, f32[4,128,128]{2,1,0:T(8,128)S(1)}, u32[]{:S(2)}, u32[]{:S(2)}) %collective-permute-start.1) | collective-permute-done | bytes 262176 | tf_op jit(solution)/shard_map/while/body/eval_jaxpr/ppermute | solution.py:16
  300.8 10.0 %collective-permute-done.1 = f32[4,128,128]{2,1,0:T(8,128)S(1)} collective-permute-done((f32[4,128,128]{2,1,0:T(8,128)S(1)}, f32[4,128,128]{2,1,0:T(8,128)S(1)}, u32[]{:S(2)}, u32[]{:S(2)}) %collective-permute-start.1) | collective-permute-done | bytes 262176 | tf_op jit(solution)/shard_map/while/body/eval_jaxpr/ppermute | solution.py:16
  312.7 11.1 %collective-permute-done.1 = f32[4,128,128]{2,1,0:T(8,128)S(1)} collective-permute-done((f32[4,128,128]{2,1,0:T(8,128)S(1)}, f32[4,128,128]{2,1,0:T(8,128)S(1)}, u32[]{:S(2)}, u32[]{:S(2)}) %collective-permute-start.1) | collective-permute-done | bytes 262176 | tf_op jit(solution)/shard_map/while/body/eval_jaxpr/ppermute | solution.py:16
  325.8 12.3 %collective-permute-done.1 = f32[4,128,128]{2,1,0:T(8,128)S(1)} collective-permute-done((f32[4,128,128]{2,1,0:T(8,128)S(1)}, f32[4,128,128]{2,1,0:T(8,128)S(1)}, u32[]{:S(2)}, u32[]{:S(2)}) %collective-permute-start.1) | collective-permute-done | bytes 262176 | tf_op jit(solution)/shard_map/while/body/eval_jaxpr/ppermute | solution.py:16
  340.1 11.6 %collective-permute-done.1 = f32[4,128,128]{2,1,0:T(8,128)S(1)} collective-permute-done((f32[4,128,128]{2,1,0:T(8,128)S(1)}, f32[4,128,128]{2,1,0:T(8,128)S(1)}, u32[]{:S(2)}, u32[]{:S(2)}) %collective-permute-start.1) | collective-permute-done | bytes 262176 | tf_op jit(solution)/shard_map/while/body/eval_jaxpr/ppermute | solution.py:16
  353.7 10.8 %collective-permute-done.1 = f32[4,128,128]{2,1,0:T(8,128)S(1)} collective-permute-done((f32[4,128,128]{2,1,0:T(8,128)S(1)}, f32[4,128,128]{2,1,0:T(8,128)S(1)}, u32[]{:S(2)}, u32[]{:S(2)}) %collective-permute-start.1) | collective-permute-done | bytes 262176 | tf_op jit(solution)/shard_map/while/body/eval_jaxpr/ppermute | solution.py:16
  366.4 9.9 %collective-permute-done.1 = f32[4,128,128]{2,1,0:T(8,128)S(1)} collective-permute-done((f32[4,128,128]{2,1,0:T(8,128)S(1)}, f32[4,128,128]{2,1,0:T(8,128)S(1)}, u32[]{:S(2)}, u32[]{:S(2)}) %collective-permute-start.1) | collective-permute-done | bytes 262176 | tf_op jit(solution)/shard_map/while/body/eval_jaxpr/ppermute | solution.py:16
  378.2 9.7 %collective-permute-done.1 = f32[4,128,128]{2,1,0:T(8,128)S(1)} collective-permute-done((f32[4,128,128]{2,1,0:T(8,128)S(1)}, f32[4,128,128]{2,1,0:T(8,128)S(1)}, u32[]{:S(2)}, u32[]{:S(2)}) %collective-permute-start.1) | collective-permute-done | bytes 262176 | tf_op jit(solution)/shard_map/while/body/eval_jaxpr/ppermute | solution.py:16
  389.8 9.7 %collective-permute-done.1 = f32[4,128,128]{2,1,0:T(8,128)S(1)} collective-permute-done((f32[4,128,128]{2,1,0:T(8,128)S(1)}, f32[4,128,128]{2,1,0:T(8,128)S(1)}, u32[]{:S(2)}, u32[]{:S(2)}) %collective-permute-start.1) | collective-permute-done | bytes 262176 | tf_op jit(solution)/shard_map/while/body/eval_jaxpr/ppermute | solution.py:16
  (129 shorter events, 190.6 us)
Async XLA Ops:
  19.5 12.4 %collective-permute-start = (f32[4,128,128]{2,1,0:T(8,128)S(1)}, f32[4,128,128]{2,1,0:T(8,128)S(1)}, u32[]{:S(2)}, u32[]{:S(2)}) collective-permute-start(f32[4,128,128]{2,1,0:T(8,128)S(1)} %add_select_fusion.4), channel_id=1, source_target_pairs={{0,8},{8,16},{16,24},{24,32},{32,40},{40,48},{48,56},{56,64},{64,7... | collective-permute-start | bytes 786440 | tf_op jit(solution)/shard_map/while/body/eval_jaxpr/ppermute | solution.py:16
  32.0 11.6 %collective-permute-start = (f32[4,128,128]{2,1,0:T(8,128)S(1)}, f32[4,128,128]{2,1,0:T(8,128)S(1)}, u32[]{:S(2)}, u32[]{:S(2)}) collective-permute-start(f32[4,128,128]{2,1,0:T(8,128)S(1)} %add_select_fusion.4), channel_id=1, source_target_pairs={{0,8},{8,16},{16,24},{24,32},{32,40},{40,48},{48,56},{56,64},{64,7... | collective-permute-start | bytes 786440 | tf_op jit(solution)/shard_map/while/body/eval_jaxpr/ppermute | solution.py:16
  43.6 11.6 %collective-permute-start = (f32[4,128,128]{2,1,0:T(8,128)S(1)}, f32[4,128,128]{2,1,0:T(8,128)S(1)}, u32[]{:S(2)}, u32[]{:S(2)}) collective-permute-start(f32[4,128,128]{2,1,0:T(8,128)S(1)} %add_select_fusion.4), channel_id=1, source_target_pairs={{0,8},{8,16},{16,24},{24,32},{32,40},{40,48},{48,56},{56,64},{64,7... | collective-permute-start | bytes 786440 | tf_op jit(solution)/shard_map/while/body/eval_jaxpr/ppermute | solution.py:16
  55.2 11.6 %collective-permute-start = (f32[4,128,128]{2,1,0:T(8,128)S(1)}, f32[4,128,128]{2,1,0:T(8,128)S(1)}, u32[]{:S(2)}, u32[]{:S(2)}) collective-permute-start(f32[4,128,128]{2,1,0:T(8,128)S(1)} %add_select_fusion.4), channel_id=1, source_target_pairs={{0,8},{8,16},{16,24},{24,32},{32,40},{40,48},{48,56},{56,64},{64,7... | collective-permute-start | bytes 786440 | tf_op jit(solution)/shard_map/while/body/eval_jaxpr/ppermute | solution.py:16
  66.8 11.6 %collective-permute-start = (f32[4,128,128]{2,1,0:T(8,128)S(1)}, f32[4,128,128]{2,1,0:T(8,128)S(1)}, u32[]{:S(2)}, u32[]{:S(2)}) collective-permute-start(f32[4,128,128]{2,1,0:T(8,128)S(1)} %add_select_fusion.4), channel_id=1, source_target_pairs={{0,8},{8,16},{16,24},{24,32},{32,40},{40,48},{48,56},{56,64},{64,7... | collective-permute-start | bytes 786440 | tf_op jit(solution)/shard_map/while/body/eval_jaxpr/ppermute | solution.py:16
  78.4 11.6 %collective-permute-start = (f32[4,128,128]{2,1,0:T(8,128)S(1)}, f32[4,128,128]{2,1,0:T(8,128)S(1)}, u32[]{:S(2)}, u32[]{:S(2)}) collective-permute-start(f32[4,128,128]{2,1,0:T(8,128)S(1)} %add_select_fusion.4), channel_id=1, source_target_pairs={{0,8},{8,16},{16,24},{24,32},{32,40},{40,48},{48,56},{56,64},{64,7... | collective-permute-start | bytes 786440 | tf_op jit(solution)/shard_map/while/body/eval_jaxpr/ppermute | solution.py:16
  90.0 12.5 %collective-permute-start = (f32[4,128,128]{2,1,0:T(8,128)S(1)}, f32[4,128,128]{2,1,0:T(8,128)S(1)}, u32[]{:S(2)}, u32[]{:S(2)}) collective-permute-start(f32[4,128,128]{2,1,0:T(8,128)S(1)} %add_select_fusion.4), channel_id=1, source_target_pairs={{0,8},{8,16},{16,24},{24,32},{32,40},{40,48},{48,56},{56,64},{64,7... | collective-permute-start | bytes 786440 | tf_op jit(solution)/shard_map/while/body/eval_jaxpr/ppermute | solution.py:16
  102.6 13.7 %collective-permute-start = (f32[4,128,128]{2,1,0:T(8,128)S(1)}, f32[4,128,128]{2,1,0:T(8,128)S(1)}, u32[]{:S(2)}, u32[]{:S(2)}) collective-permute-start(f32[4,128,128]{2,1,0:T(8,128)S(1)} %add_select_fusion.4), channel_id=1, source_target_pairs={{0,8},{8,16},{16,24},{24,32},{32,40},{40,48},{48,56},{56,64},{64,7... | collective-permute-start | bytes 786440 | tf_op jit(solution)/shard_map/while/body/eval_jaxpr/ppermute | solution.py:16
  116.4 13.9 %collective-permute-start = (f32[4,128,128]{2,1,0:T(8,128)S(1)}, f32[4,128,128]{2,1,0:T(8,128)S(1)}, u32[]{:S(2)}, u32[]{:S(2)}) collective-permute-start(f32[4,128,128]{2,1,0:T(8,128)S(1)} %add_select_fusion.4), channel_id=1, source_target_pairs={{0,8},{8,16},{16,24},{24,32},{32,40},{40,48},{48,56},{56,64},{64,7... | collective-permute-start | bytes 786440 | tf_op jit(solution)/shard_map/while/body/eval_jaxpr/ppermute | solution.py:16
  130.3 13.1 %collective-permute-start = (f32[4,128,128]{2,1,0:T(8,128)S(1)}, f32[4,128,128]{2,1,0:T(8,128)S(1)}, u32[]{:S(2)}, u32[]{:S(2)}) collective-permute-start(f32[4,128,128]{2,1,0:T(8,128)S(1)} %add_select_fusion.4), channel_id=1, source_target_pairs={{0,8},{8,16},{16,24},{24,32},{32,40},{40,48},{48,56},{56,64},{64,7... | collective-permute-start | bytes 786440 | tf_op jit(solution)/shard_map/while/body/eval_jaxpr/ppermute | solution.py:16
  143.5 12.2 %collective-permute-start = (f32[4,128,128]{2,1,0:T(8,128)S(1)}, f32[4,128,128]{2,1,0:T(8,128)S(1)}, u32[]{:S(2)}, u32[]{:S(2)}) collective-permute-start(f32[4,128,128]{2,1,0:T(8,128)S(1)} %add_select_fusion.4), channel_id=1, source_target_pairs={{0,8},{8,16},{16,24},{24,32},{32,40},{40,48},{48,56},{56,64},{64,7... | collective-permute-start | bytes 786440 | tf_op jit(solution)/shard_map/while/body/eval_jaxpr/ppermute | solution.py:16
  155.8 11.6 %collective-permute-start = (f32[4,128,128]{2,1,0:T(8,128)S(1)}, f32[4,128,128]{2,1,0:T(8,128)S(1)}, u32[]{:S(2)}, u32[]{:S(2)}) collective-permute-start(f32[4,128,128]{2,1,0:T(8,128)S(1)} %add_select_fusion.4), channel_id=1, source_target_pairs={{0,8},{8,16},{16,24},{24,32},{32,40},{40,48},{48,56},{56,64},{64,7... | collective-permute-start | bytes 786440 | tf_op jit(solution)/shard_map/while/body/eval_jaxpr/ppermute | solution.py:16
  167.4 11.6 %collective-permute-start = (f32[4,128,128]{2,1,0:T(8,128)S(1)}, f32[4,128,128]{2,1,0:T(8,128)S(1)}, u32[]{:S(2)}, u32[]{:S(2)}) collective-permute-start(f32[4,128,128]{2,1,0:T(8,128)S(1)} %add_select_fusion.4), channel_id=1, source_target_pairs={{0,8},{8,16},{16,24},{24,32},{32,40},{40,48},{48,56},{56,64},{64,7... | collective-permute-start | bytes 786440 | tf_op jit(solution)/shard_map/while/body/eval_jaxpr/ppermute | solution.py:16
  179.0 11.6 %collective-permute-start = (f32[4,128,128]{2,1,0:T(8,128)S(1)}, f32[4,128,128]{2,1,0:T(8,128)S(1)}, u32[]{:S(2)}, u32[]{:S(2)}) collective-permute-start(f32[4,128,128]{2,1,0:T(8,128)S(1)} %add_select_fusion.4), channel_id=1, source_target_pairs={{0,8},{8,16},{16,24},{24,32},{32,40},{40,48},{48,56},{56,64},{64,7... | collective-permute-start | bytes 786440 | tf_op jit(solution)/shard_map/while/body/eval_jaxpr/ppermute | solution.py:16
  213.5 14.2 %collective-permute-start.1 = (f32[4,128,128]{2,1,0:T(8,128)S(1)}, f32[4,128,128]{2,1,0:T(8,128)S(1)}, u32[]{:S(2)}, u32[]{:S(2)}) collective-permute-start(f32[4,128,128]{2,1,0:T(8,128)S(1)} %add_select_fusion.5), channel_id=1, source_target_pairs={{8,0},{16,8},{24,16},{32,24},{40,32},{48,40},{56,48},{64,56},{72,6... | collective-permute-start | bytes 786440 | tf_op jit(solution)/shard_map/while/body/eval_jaxpr/ppermute | solution.py:16
  227.7 12.7 %collective-permute-start.1 = (f32[4,128,128]{2,1,0:T(8,128)S(1)}, f32[4,128,128]{2,1,0:T(8,128)S(1)}, u32[]{:S(2)}, u32[]{:S(2)}) collective-permute-start(f32[4,128,128]{2,1,0:T(8,128)S(1)} %add_select_fusion.5), channel_id=1, source_target_pairs={{8,0},{16,8},{24,16},{32,24},{40,32},{48,40},{56,48},{64,56},{72,6... | collective-permute-start | bytes 786440 | tf_op jit(solution)/shard_map/while/body/eval_jaxpr/ppermute | solution.py:16
  240.5 11.8 %collective-permute-start.1 = (f32[4,128,128]{2,1,0:T(8,128)S(1)}, f32[4,128,128]{2,1,0:T(8,128)S(1)}, u32[]{:S(2)}, u32[]{:S(2)}) collective-permute-start(f32[4,128,128]{2,1,0:T(8,128)S(1)} %add_select_fusion.5), channel_id=1, source_target_pairs={{8,0},{16,8},{24,16},{32,24},{40,32},{48,40},{56,48},{64,56},{72,6... | collective-permute-start | bytes 786440 | tf_op jit(solution)/shard_map/while/body/eval_jaxpr/ppermute | solution.py:16
  264.0 11.6 %collective-permute-start.1 = (f32[4,128,128]{2,1,0:T(8,128)S(1)}, f32[4,128,128]{2,1,0:T(8,128)S(1)}, u32[]{:S(2)}, u32[]{:S(2)}) collective-permute-start(f32[4,128,128]{2,1,0:T(8,128)S(1)} %add_select_fusion.5), channel_id=1, source_target_pairs={{8,0},{16,8},{24,16},{32,24},{40,32},{48,40},{56,48},{64,56},{72,6... | collective-permute-start | bytes 786440 | tf_op jit(solution)/shard_map/while/body/eval_jaxpr/ppermute | solution.py:16
  298.8 12.0 %collective-permute-start.1 = (f32[4,128,128]{2,1,0:T(8,128)S(1)}, f32[4,128,128]{2,1,0:T(8,128)S(1)}, u32[]{:S(2)}, u32[]{:S(2)}) collective-permute-start(f32[4,128,128]{2,1,0:T(8,128)S(1)} %add_select_fusion.5), channel_id=1, source_target_pairs={{8,0},{16,8},{24,16},{32,24},{40,32},{48,40},{56,48},{64,56},{72,6... | collective-permute-start | bytes 786440 | tf_op jit(solution)/shard_map/while/body/eval_jaxpr/ppermute | solution.py:16
  310.8 13.1 %collective-permute-start.1 = (f32[4,128,128]{2,1,0:T(8,128)S(1)}, f32[4,128,128]{2,1,0:T(8,128)S(1)}, u32[]{:S(2)}, u32[]{:S(2)}) collective-permute-start(f32[4,128,128]{2,1,0:T(8,128)S(1)} %add_select_fusion.5), channel_id=1, source_target_pairs={{8,0},{16,8},{24,16},{32,24},{40,32},{48,40},{56,48},{64,56},{72,6... | collective-permute-start | bytes 786440 | tf_op jit(solution)/shard_map/while/body/eval_jaxpr/ppermute | solution.py:16
  323.9 14.2 %collective-permute-start.1 = (f32[4,128,128]{2,1,0:T(8,128)S(1)}, f32[4,128,128]{2,1,0:T(8,128)S(1)}, u32[]{:S(2)}, u32[]{:S(2)}) collective-permute-start(f32[4,128,128]{2,1,0:T(8,128)S(1)} %add_select_fusion.5), channel_id=1, source_target_pairs={{8,0},{16,8},{24,16},{32,24},{40,32},{48,40},{56,48},{64,56},{72,6... | collective-permute-start | bytes 786440 | tf_op jit(solution)/shard_map/while/body/eval_jaxpr/ppermute | solution.py:16
  338.1 13.5 %collective-permute-start.1 = (f32[4,128,128]{2,1,0:T(8,128)S(1)}, f32[4,128,128]{2,1,0:T(8,128)S(1)}, u32[]{:S(2)}, u32[]{:S(2)}) collective-permute-start(f32[4,128,128]{2,1,0:T(8,128)S(1)} %add_select_fusion.5), channel_id=1, source_target_pairs={{8,0},{16,8},{24,16},{32,24},{40,32},{48,40},{56,48},{64,56},{72,6... | collective-permute-start | bytes 786440 | tf_op jit(solution)/shard_map/while/body/eval_jaxpr/ppermute | solution.py:16
  351.7 12.7 %collective-permute-start.1 = (f32[4,128,128]{2,1,0:T(8,128)S(1)}, f32[4,128,128]{2,1,0:T(8,128)S(1)}, u32[]{:S(2)}, u32[]{:S(2)}) collective-permute-start(f32[4,128,128]{2,1,0:T(8,128)S(1)} %add_select_fusion.5), channel_id=1, source_target_pairs={{8,0},{16,8},{24,16},{32,24},{40,32},{48,40},{56,48},{64,56},{72,6... | collective-permute-start | bytes 786440 | tf_op jit(solution)/shard_map/while/body/eval_jaxpr/ppermute | solution.py:16
  364.5 11.8 %collective-permute-start.1 = (f32[4,128,128]{2,1,0:T(8,128)S(1)}, f32[4,128,128]{2,1,0:T(8,128)S(1)}, u32[]{:S(2)}, u32[]{:S(2)}) collective-permute-start(f32[4,128,128]{2,1,0:T(8,128)S(1)} %add_select_fusion.5), channel_id=1, source_target_pairs={{8,0},{16,8},{24,16},{32,24},{40,32},{48,40},{56,48},{64,56},{72,6... | collective-permute-start | bytes 786440 | tf_op jit(solution)/shard_map/while/body/eval_jaxpr/ppermute | solution.py:16
  (20 other events, 659.5 us)
where the time goes:
time: 411 us; the launch traced here: 410 us
  waiting for transfers between devices  224 us (55%)
  starting transfers between devices  142 us (35%)
  blocking collectives  12.4 us (3%)
  local copies, waits for them, and re-layouts  10.1 us (2%)
  matrix products  10.1 us (2%)
  other arithmetic  6.93 us (2%)
    ppermute x30, waiting for transfers between devices, shifted(): lax.ppermute(value, axis, [(source, source + steps) for source in range(f...  224 us
    ppermute x30, starting transfers between devices, shifted(): lax.ppermute(value, axis, [(source, source + steps) for source in range(f...  142 us
    psum x1, blocking collectives, on_device(): lax.psum((jnp.sum(attended * attended, axis=(1, 2)), jnp.sum(attended * s...  12.4 us
  transfers between devices with their start and end apart: 30, of which 30 were waited for; matrix products, arithmetic and copies ran while one was open for 0% of the time, Pallas kernels for 0%

commit v1 on v0

v1 whole, which is shorter than its diff:
```python
import functools

import jax
import jax.numpy as jnp
from jax import lax
from jax.experimental import pallas as pl
from jax.experimental.pallas import tpu as pltpu
from jax.sharding import PartitionSpec as P

DH = 128
WIDTH = 4096
EPSILON = 1e-06
QUARTERS = 4
LOADS = 4

F32 = jnp.float32
BF16 = jnp.bfloat16
I32 = jnp.int32


def dot(a, b, contract):
    return lax.dot_general(a, b, ((contract[:1], contract[1:]), ((), ())), preferred_element_type=F32)


def heads_of(array):
    return [slice(h * DH, (h + 1) * DH) for h in range(array.shape[-1] // DH)]


def row_index(rows):
    return lax.broadcasted_iota(I32, (rows, DH), 0)


def kv_kernel(per, starts_hbm, k_hbm, v_hbm, state_ref, bounds_ref, ends_ref, flags_ref, starts, k_buf, v_buf, sems):
    rows, width = k_buf.shape
    step = rows // LOADS
    starts_copy = pltpu.make_async_copy(starts_hbm, starts, sems.at[0])
    starts_copy.start()
    loads = []
    for i in range(LOADS):
        part = pl.ds(i * step, step)
        loads.append(pltpu.make_async_copy(k_hbm.at[part], k_buf.at[part], sems.at[1 + 2 * i]))
        loads.append(pltpu.make_async_copy(v_hbm.at[part], v_buf.at[part], sems.at[2 + 2 * i]))
    for load in loads:
        load.start()
    pos = lax.axis_index("seq")
    first = pos * rows
    quarter_first = (pos // per) * per * rows
    block = quarter_first + rows * lax.broadcasted_iota(I32, (per, DH), 0)
    column = lax.broadcasted_iota(I32, ends_ref.shape, 1)
    starts_copy.wait()
    head_end = jnp.full((4, DH), rows, I32)
    tail_start = jnp.full((4, DH), 0, I32)
    ends = jnp.full(ends_ref.shape, rows, I32)
    yes = jnp.ones((per, DH), F32)
    no = jnp.zeros((per, DH), F32)
    keep_forward, take_forward, keep_backward, take_backward = yes, yes, yes, yes
    for i in range(starts_hbm.shape[0] - 1, -1, -1):
        start = starts[i]
        here = start - first
        head_end = jnp.where(here > 0, jnp.minimum(head_end, here), head_end)
        tail_start = jnp.where(here < rows, jnp.maximum(tail_start, here), tail_start)
        ends = jnp.where(column < here, jnp.minimum(ends, here), ends)
        offset = start - block
        inside = (offset > 0) & (offset < rows)
        keep_forward = jnp.where(inside | (offset == rows), no, keep_forward)
        take_forward = jnp.where(offset == rows, no, take_forward)
        keep_backward = jnp.where(inside | (offset == 0), no, keep_backward)
        take_backward = jnp.where(offset == 0, no, take_backward)
    bounds_ref[0:4] = head_end
    bounds_ref[4:8] = tail_start
    ends_ref[...] = ends
    for i, flag in enumerate((keep_forward, take_forward, keep_backward, take_backward)):
        flags_ref[i] = flag
    half = rows // 2
    for j in range(2):
        for load in loads[j * LOADS : (j + 1) * LOADS]:
            load.wait()
        part = slice(j * half, (j + 1) * half)
        chosen = row_index(half) + j * half >= tail_start[:1]
        for h, cols in enumerate(heads_of(k_buf)):
            k = jnp.where(chosen, k_buf[part, cols], jnp.zeros((), BF16))
            term = dot(k, v_buf[part, cols], (0, 0))
            state_ref[h] = term if j == 0 else state_ref[h] + term


def scan_kernel(backward, flags_ref, x_ref, out_ref):
    count = x_ref.shape[0]
    order = list(range(count))[:: -1 if backward else 1]
    keep, take = (2, 3) if backward else (0, 1)
    running = jnp.zeros(x_ref.shape[1:], F32)
    out_ref[order[0]] = running
    for b, later in zip(order[:-1], order[1:]):
        running = running * flags_ref[keep, b : b + 1] + x_ref[b] * flags_ref[take, b : b + 1]
        out_ref[later] = running


def allowed_mask(ends_ref):
    rows = ends_ref.shape[1]
    row = lax.broadcasted_iota(I32, (rows, rows), 0)
    return (lax.broadcasted_iota(I32, (rows, rows), 1) <= row) & (row < ends_ref[0:1])


def intra_kernel(bounds_ref, ends_ref, q_ref, k_ref, v_ref, g_ref, gain_ref, scores_ref, intra_ref, scaled_ref, head_ref, turned_ref):
    rows = q_ref.shape[0]
    from_head = row_index(rows) < bounds_ref[0:1]
    allowed = allowed_mask(ends_ref)
    for h, cols in enumerate(heads_of(q_ref)):
        scores = dot(q_ref[:, cols], k_ref[:, cols], (1, 1))
        masked = jnp.where(allowed, scores, 0.0).astype(BF16)
        scores_ref[h] = masked
        intra_ref[:, cols] = dot(masked, v_ref[:, cols], (1, 0))
        scaled_ref[:, cols] = gain_ref[:, cols] * g_ref[:, cols].astype(F32)
        head = jnp.where(from_head, q_ref[:, cols], jnp.zeros((), BF16))
        head_ref[:, cols] = head
        turned_ref[h] = head.T


def attend_kernel(head_ref, intra_ref, prefix_ref, scaled_ref, attended_ref, sums_ref):
    rows = head_ref.shape[0]
    squares = jnp.zeros((rows, DH), F32)
    crosses = jnp.zeros((rows, DH), F32)
    for h, cols in enumerate(heads_of(head_ref)):
        attended = intra_ref[:, cols] + dot(head_ref[:, cols], prefix_ref[h].astype(BF16), (1, 0))
        attended_ref[:, cols] = attended
        squares += attended * attended
        crosses += attended * scaled_ref[:, cols]
    parts = rows // DH
    for i in range(parts):
        part = slice(i * DH, (i + 1) * DH)
        square = jnp.sum(squares[part].T, axis=0, keepdims=True)
        cross = jnp.sum(crosses[part].T, axis=0, keepdims=True)
        for to in range(sums_ref.shape[0]):
            sums_ref[to, i : i + 1] = square
            sums_ref[to, parts + i : parts + i + 1] = cross


def grad_kernel(turned_ref, attended_ref, scaled_ref, sums_ref, normed_ref, state_ref):
    rows = attended_ref.shape[0]
    parts = rows // DH
    sums = jnp.sum(sums_ref[...], axis=0)
    inverse = lax.rsqrt(sums[:parts] / WIDTH + EPSILON)
    factor = inverse * inverse * inverse * (sums[parts:] / WIDTH)
    for i in range(parts):
        part = slice(i * DH, (i + 1) * DH)
        inverse_here = jnp.broadcast_to(inverse[i : i + 1], (DH, DH)).T
        factor_here = jnp.broadcast_to(factor[i : i + 1], (DH, DH)).T
        for cols in heads_of(attended_ref):
            normed = scaled_ref[part, cols] * inverse_here - attended_ref[part, cols] * factor_here
            normed_ref[part, cols] = normed.astype(BF16)
    for h, cols in enumerate(heads_of(attended_ref)):
        state_ref[h] = dot(turned_ref[h], normed_ref[:, cols], (1, 0))


def products_kernel(bounds_ref, ends_ref, q_ref, k_ref, v_ref, normed_ref, prefix_ref, scores_ref, dq_ref, dk_ref, dv_ref):
    rows = q_ref.shape[0]
    from_head = row_index(rows) < bounds_ref[0:1]
    allowed = allowed_mask(ends_ref)
    for h, cols in enumerate(heads_of(q_ref)):
        normed = normed_ref[:, cols]
        products = dot(normed, v_ref[:, cols], (1, 1))
        products = jnp.where(allowed, products, 0.0).astype(BF16)
        carried = dot(normed, prefix_ref[h].astype(BF16), (1, 1))
        dq = dot(products, k_ref[:, cols], (1, 0)) + jnp.where(from_head, carried, 0.0)
        dq_ref[:, cols] = dq.astype(BF16)
        dk_ref[:, cols] = dot(products, q_ref[:, cols], (0, 0))
        dv_ref[:, cols] = dot(scores_ref[h], normed, (0, 0))


def final_kernel(bounds_ref, k_ref, v_ref, dk_ref, dv_ref, later_ref, key_hbm, value_hbm, key_buf, value_buf, sems):
    rows = k_ref.shape[0]
    to_tail = row_index(rows) >= bounds_ref[4:5]
    stores = []
    for h, cols in enumerate(heads_of(k_ref)):
        later = later_ref[h].astype(BF16)
        dk = dot(v_ref[:, cols], later, (1, 1))
        key_buf[:, cols] = (dk_ref[:, cols] + jnp.where(to_tail, dk, 0.0)).astype(BF16)
        stores.append(pltpu.make_async_copy(key_buf.at[:, cols], key_hbm.at[:, cols], sems.at[2 * h]))
        stores[-1].start()
        dv = dot(k_ref[:, cols], later, (1, 0))
        value_buf[:, cols] = (dv_ref[:, cols] + jnp.where(to_tail, dv, 0.0)).astype(BF16)
        stores.append(pltpu.make_async_copy(value_buf.at[:, cols], value_hbm.at[:, cols], sems.at[2 * h + 1]))
        stores[-1].start()
    for store in stores:
        store.wait()


HBM = pl.BlockSpec(memory_space=pltpu.HBM)
VMEM = pl.BlockSpec(memory_space=pltpu.VMEM)


def call(kernel, arrays, outs, flops, name, in_specs=None, out_spec=VMEM, scratch=()):
    out_shape = tuple(jax.ShapeDtypeStruct(s, d) for s, d in outs)
    moved = sum(a.size * a.dtype.itemsize for a in arrays) + sum(o.size * o.dtype.itemsize for o in out_shape)
    return pl.pallas_call(
        kernel,
        out_shape=out_shape,
        in_specs=in_specs or [VMEM] * len(arrays),
        out_specs=(out_spec,) * len(outs),
        scratch_shapes=list(scratch),
        compiler_params=pltpu.CompilerParams(vmem_limit_bytes=16 * 1024 * 1024),
        cost_estimate=pl.CostEstimate(flops=flops, bytes_accessed=moved, transcendentals=0),
        name=name,
    )(*arrays)


def on_device(queries, keys, values, out_grad, gain, doc_starts):
    rows, width = queries.shape
    heads = width // DH
    per = lax.axis_size("seq") // QUARTERS
    head_devices = lax.axis_size("head")
    gain_row = gain.reshape(1, width)
    groups = [[g * per + i for i in range(per)] for g in range(QUARTERS)]
    state_shape = (heads, DH, DH)
    pieces = (per, heads * DH // per, DH)
    state_flops = 2 * rows * width * DH
    full_flops = 2 * rows * rows * width
    whole = (rows, width)

    def swap(x):
        return lax.all_to_all(x.reshape(pieces), "seq", 0, 0, axis_index_groups=groups, tiled=True)

    def scan(state, flags, backward):
        (mine,) = call(functools.partial(scan_kernel, backward), (flags, swap(state)), [(pieces, F32)], 0, "state_scan")
        return swap(mine).reshape(state_shape)

    kv_state, bounds, ends, flags = call(
        functools.partial(kv_kernel, per),
        (doc_starts, keys, values),
        [(state_shape, F32), ((8, DH), I32), ((8, rows), I32), ((4, per, DH), F32)],
        state_flops,
        "kv_state",
        in_specs=[HBM] * 3,
        scratch=[
            pltpu.SMEM(doc_starts.shape, I32),
            pltpu.VMEM(whole, BF16),
            pltpu.VMEM(whole, BF16),
            pltpu.SemaphoreType.DMA((1 + 2 * LOADS,)),
        ],
    )
    prefix = scan(kv_state, flags, False)
    scores, intra, scaled, head, turned = call(
        intra_kernel,
        (bounds, ends, queries, keys, values, out_grad, gain_row),
        [((heads, rows, rows), BF16), (whole, F32), (whole, F32), (whole, BF16), ((heads, DH, rows), BF16)],
        2 * full_flops,
        "intra",
    )
    attended, sums = call(
        attend_kernel,
        (head, intra, prefix, scaled),
        [(whole, F32), ((head_devices, 2 * rows // DH, DH), F32)],
        state_flops,
        "attend",
    )
    sums = lax.all_to_all(sums, "head", 0, 0, tiled=True)
    normed, grad_state = call(
        grad_kernel,
        (turned, attended, scaled, sums),
        [(whole, BF16), (state_shape, F32)],
        state_flops,
        "normed_grad",
    )
    later = scan(grad_state, flags, True)
    query_grad, key_part, value_part = call(
        products_kernel,
        (bounds, ends, queries, keys, values, normed, prefix, scores),
        [(whole, BF16), (whole, F32), (whole, F32)],
        4 * full_flops + state_flops,
        "products",
    )
    key_grad, value_grad = call(
        final_kernel,
        (bounds, keys, values, key_part, value_part, later),
        [(whole, BF16), (whole, BF16)],
        2 * state_flops,
        "key_value_grad",
        out_spec=HBM,
        scratch=[
            pltpu.VMEM(whole, BF16),
            pltpu.VMEM(whole, BF16),
            pltpu.SemaphoreType.DMA((2 * heads,)),
        ],
    )
    return query_grad, key_grad, value_grad


def solution(mesh):
    placed = (P("seq", "head"),) * 4 + (P("head"), P())
    return jax.shard_map(
        on_device,
        mesh=mesh,
        in_specs=placed,
        out_specs=(P("seq", "head"),) * 3,
        check_vma=False,
    )
```

time: 411 us -> 86 us (0.21)
  the two profiles are of different devices: /device:TPU:248 before, /device:TPU:136 now
where the time goes in v1:
time: 86 us; the launch traced here: 85.3 us
  blocking collectives  42.9 us (50%)
  local copies, waits for them, and re-layouts  14.6 us (17%)
  Pallas kernels  10.6 us (12%)
  starting transfers between devices  9.12 us (11%)
  waiting for transfers between devices  7.36 us (9%)
    all_to_all x2, blocking collectives, swap(): lax.all_to_all(x.reshape(pieces), 'seq', 0, 0, axis_index_groups=groups,...  33.4 us
    unnamed x40, local copies, waits for them, and re-layouts  14.6 us
    pallas_call x8, Pallas kernels, call(): pl.pallas_call(kernel, out_shape=out_shape, in_specs=in_specs or [VMEM] *...  10.6 us
    all_to_all x1, blocking collectives, on_device(): sums = lax.all_to_all(sums, 'head', 0, 0, tiled=True)  9.54 us
    all_to_all x2, starting transfers between devices, swap(): lax.all_to_all(x.reshape(pieces), 'seq', 0, 0, axis_index_groups=groups,...  9.12 us
    all_to_all x2, waiting for transfers between devices, swap(): lax.all_to_all(x.reshape(pieces), 'seq', 0, 0, axis_index_groups=groups,...  7.36 us
  transfers between devices with their start and end apart: 2, of which 2 were waited for; matrix products, arithmetic and copies ran while one was open for 0% of the time, Pallas kernels for 5%

profile of v1, /device:TPU:136, one launch (start us, length us, event | category | flops | bytes accessed | tf_op | source)
XLA Modules:
  0.0 85.3 jit_solution(12910026941448274825)
XLA Ops:
  0.6 1.0 %copy-done = bf16[512,512]{1,0:T(8,128)(2,1)S(1)} copy-done((bf16[512,512]{1,0:T(8,128)(2,1)S(1)}, bf16[512,512]{1,0:T(8,128)(2,1)}, u32[]{:S(2)}) %copy-start) | copy-done | bytes 524312
  1.7 1.0 %copy-done.2 = bf16[512,512]{1,0:T(8,128)(2,1)S(1)} copy-done((bf16[512,512]{1,0:T(8,128)(2,1)S(1)}, bf16[512,512]{1,0:T(8,128)(2,1)}, u32[]{:S(2)}) %copy-start.2) | copy-done | bytes 524312
  3.4 2.2 %kv_state.1 = (f32[4,128,128]{2,1,0:T(8,128)S(1)}, s32[8,128]{1,0:T(8,128)S(1)}, s32[8,512]{1,0:T(8,128)S(1)}, f32[4,16,128]{2,1,0:T(8,128)S(1)}) custom-call(s32[25]{0:T(128)S(1)} %copy-done.19, bf16[512,512]{1,0:T(8,128)(2,1)S(1)} %copy-done, bf16[512,512]{1,0:T(8,128)(2,1)S(1)} %copy-done.2), custom_call_target="tpu_custom_call" | custom-call | flops 67108864 | bytes 1364068 | tf_op jit(solution)/shard_map/kv_state/pallas_call | solution.py:194
  5.6 19.2 %all_to_all.25.x_ref = f32[16,32,128]{2,1,0:T(8,128)S(1)} all-to-all(f32[16,32,128]{2,1,0:T(8,128)S(1)} %bitcast.9), channel_id=1, replica_groups={{0,8,16,24,32,40,48,56,64,72,80,88,96,104,112,120},{128,136,144,152,160..., dimensions={0} | all-to-all | bytes 524288 | tf_op jit(solution)/shard_map/all_to_all | solution.py:220
  25.6 4.6 %all-to-all-start.1 = ((f32[16,32,128]{2,1,0:T(8,128)}), f32[16,32,128]{2,1,0:T(8,128)S(1)}, u32[]{:S(2)}, u32[]{:S(2)}) async-start(f32[16,32,128]{2,1,0:T(8,128)} %state_scan.2), calls=%async_computation.1 | async-start | bytes 524288 | tf_op jit(solution)/shard_map/all_to_all | solution.py:220
  30.2 1.4 %intra.1 = (bf16[4,512,512]{2,1,0:T(8,128)(2,1)S(1)}, f32[512,512]{1,0:T(8,128)S(1)}, f32[512,512]{1,0:T(8,128)S(1)}, bf16[512,512]{1,0:T(8,128)(2,1)S(1)}, bf16[4,128,512]{2,1,0:T(8,128)(2,1)S(1)}) custom-call(s32[8,128]{1,0:T(8,128)S(1)} %get-tuple-element.21.bounds_ref, s32[8,512]{1,0:T(8,128)S(1)} %get-tuple-element.22.ends_ref, ...), custom_call_target="tpu_custom_call" | custom-call | flops 536870912 | bytes 7362560 | tf_op jit(solution)/shard_map/intra/pallas_call | solution.py:194
  31.7 1.3 %copy-done.5 = bf16[4,512,512]{2,1,0:T(8,128)(2,1)} copy-done((bf16[4,512,512]{2,1,0:T(8,128)(2,1)}, bf16[4,512,512]{2,1,0:T(8,128)(2,1)S(1)}, u32[]{:S(2)}) %copy-start.5) | copy-done | bytes 2097176
  33.0 1.0 %copy-done.9 = f32[512,512]{1,0:T(8,128)} copy-done((f32[512,512]{1,0:T(8,128)}, f32[512,512]{1,0:T(8,128)S(1)}, u32[]{:S(2)}) %copy-start.9) | copy-done | bytes 1048600
  34.0 0.8 copy-done.14
  34.8 0.8 copy-done.16
  35.6 4.4 %all-to-all-done.1 = f32[16,32,128]{2,1,0:T(8,128)S(1)} async-done(((f32[16,32,128]{2,1,0:T(8,128)}), f32[16,32,128]{2,1,0:T(8,128)S(1)}, u32[]{:S(2)}, u32[]{:S(2)}) %all-to-all-start.1) | async-done | bytes 262176 | tf_op jit(solution)/shard_map/all_to_all | solution.py:220
  40.0 1.2 %copy-done.10 = f32[512,512]{1,0:T(8,128)S(1)} copy-done((f32[512,512]{1,0:T(8,128)S(1)}, f32[512,512]{1,0:T(8,128)}, u32[]{:S(2)}) %copy-start.10) | copy-done | bytes 1048600
  41.2 1.0 %copy-done.17 = bf16[512,512]{1,0:T(8,128)(2,1)S(1)} copy-done((bf16[512,512]{1,0:T(8,128)(2,1)S(1)}, bf16[512,512]{1,0:T(8,128)(2,1)}, u32[]{:S(2)}) %copy-start.17) | copy-done | bytes 524312
  42.7 9.5 %all_to_all.26.sums_ref = f32[8,8,128]{2,1,0:T(8,128)S(1)} all-to-all(f32[8,8,128]{2,1,0:T(8,128)S(1)} %get-tuple-element.30), channel_id=1, replica_groups=mesh['seq'=64,'head'=8] {'head'}, dimensions={0} | all-to-all | bytes 65536 | tf_op jit(solution)/shard_map/all_to_all | solution.py:255
  52.8 0.8 copy-done.12
  53.6 14.1 %all_to_all.27.x_ref = f32[16,32,128]{2,1,0:T(8,128)S(1)} all-to-all(f32[16,32,128]{2,1,0:T(8,128)S(1)} %bitcast.8), channel_id=1, replica_groups={{0,8,16,24,32,40,48,56,64,72,80,88,96,104,112,120},{128,136,144,152,160..., dimensions={0} | all-to-all | bytes 524288 | tf_op jit(solution)/shard_map/all_to_all | solution.py:220
  68.5 4.5 %all-to-all-start.4 = ((f32[16,32,128]{2,1,0:T(8,128)}), f32[16,32,128]{2,1,0:T(8,128)S(1)}, u32[]{:S(2)}, u32[]{:S(2)}) async-start(f32[16,32,128]{2,1,0:T(8,128)} %state_scan.3), calls=%async_computation.4 | async-start | bytes 524288 | tf_op jit(solution)/shard_map/all_to_all | solution.py:220
  73.0 1.6 %copy-done.6 = bf16[4,512,512]{2,1,0:T(8,128)(2,1)S(1)} copy-done((bf16[4,512,512]{2,1,0:T(8,128)(2,1)S(1)}, bf16[4,512,512]{2,1,0:T(8,128)(2,1)}, u32[]{:S(2)}) %copy-start.6) | copy-done | bytes 2097176
  74.6 1.0 %copy-done.13 = bf16[512,512]{1,0:T(8,128)(2,1)S(1)} copy-done((bf16[512,512]{1,0:T(8,128)(2,1)S(1)}, bf16[512,512]{1,0:T(8,128)(2,1)}, u32[]{:S(2)}) %copy-start.13) | copy-done | bytes 524312
  75.6 3.2 %products.1 = (bf16[512,512]{1,0:T(8,128)(2,1)}, f32[512,512]{1,0:T(8,128)S(1)}, f32[512,512]{1,0:T(8,128)S(1)}) custom-call(s32[8,128]{1,0:T(8,128)S(1)} %get-tuple-element.21.bounds_ref, s32[8,512]{1,0:T(8,128)S(1)} %get-tuple-element.22.ends_ref, bf16[512,512]{1,0:T(8,128)(2,1)S(1)} %copy-done.4, bf16[512,512]{1,0:T(8,128)(2,1)S(1)} %copy-done.1, ...), custom_call_target="tpu_custom_call" | custom-call | flops 1140850688 | bytes 7098368 | tf_op jit(solution)/shard_map/products/pallas_call | solution.py:194
  78.9 1.0 %copy-done.7 = f32[512,512]{1,0:T(8,128)} copy-done((f32[512,512]{1,0:T(8,128)}, f32[512,512]{1,0:T(8,128)S(1)}, u32[]{:S(2)}) %copy-start.7) | copy-done | bytes 1048600
  79.9 3.0 %all-to-all-done.4 = f32[16,32,128]{2,1,0:T(8,128)S(1)} async-done(((f32[16,32,128]{2,1,0:T(8,128)}), f32[16,32,128]{2,1,0:T(8,128)S(1)}, u32[]{:S(2)}, u32[]{:S(2)}) %all-to-all-start.4) | async-done | bytes 262176 | tf_op jit(solution)/shard_map/all_to_all | solution.py:220
  82.8 1.2 %copy-done.8 = f32[512,512]{1,0:T(8,128)S(1)} copy-done((f32[512,512]{1,0:T(8,128)S(1)}, f32[512,512]{1,0:T(8,128)}, u32[]{:S(2)}) %copy-start.8) | copy-done | bytes 1048600
  84.0 1.3 %key_value_grad.1 = (bf16[512,512]{1,0:T(8,128)(2,1)}, bf16[512,512]{1,0:T(8,128)(2,1)}) custom-call(s32[8,128]{1,0:T(8,128)S(1)} %get-tuple-element.21.bounds_ref, bf16[512,512]{1,0:T(8,128)(2,1)S(1)} %copy-done.1, bf16[512,512]{1,0:T(8,128)(2,1)S(1)} %copy-done.3, f32[512,512]{1,0:T(8,128)S(1)} %get-tuple-element.34.dk_ref, f32[512,512]{1,0:T(8,128)S(1)} %copy-done.8, ...), custom_call_target="tpu_custom_call" | custom-call | flops 134217728 | bytes 4460544 | tf_op jit(solution)/shard_map/key_value_grad/pallas_call | solution.py:194
  (31 shorter events, 3.2 us)
Async XLA Ops:
  0.6 1.0 %copy-start = (bf16[512,512]{1,0:T(8,128)(2,1)S(1)}, bf16[512,512]{1,0:T(8,128)(2,1)}, u32[]{:S(2)}) copy-start(bf16[512,512]{1,0:T(8,128)(2,1)} %k_ref.5) | copy-start | bytes 1572868
  1.7 1.0 %copy-start.2 = (bf16[512,512]{1,0:T(8,128)(2,1)S(1)}, bf16[512,512]{1,0:T(8,128)(2,1)}, u32[]{:S(2)}) copy-start(bf16[512,512]{1,0:T(8,128)(2,1)} %v_ref.5) | copy-start | bytes 1572868
  2.7 0.7 copy-start.19
  3.4 26.8 %copy-start.1 = (bf16[512,512]{1,0:T(8,128)(2,1)S(1)}, bf16[512,512]{1,0:T(8,128)(2,1)}, u32[]{:S(2)}) copy-start(bf16[512,512]{1,0:T(8,128)(2,1)} %k_ref.5) | copy-start | bytes 1572868
  3.4 26.8 %copy-start.3 = (bf16[512,512]{1,0:T(8,128)(2,1)S(1)}, bf16[512,512]{1,0:T(8,128)(2,1)}, u32[]{:S(2)}) copy-start(bf16[512,512]{1,0:T(8,128)(2,1)} %v_ref.5) | copy-start | bytes 1572868
  3.4 26.8 %copy-start.4 = (bf16[512,512]{1,0:T(8,128)(2,1)S(1)}, bf16[512,512]{1,0:T(8,128)(2,1)}, u32[]{:S(2)}) copy-start(bf16[512,512]{1,0:T(8,128)(2,1)} %q_ref.3) | copy-start | bytes 1572868
  3.4 26.8 %copy-start.11 = (bf16[512,512]{1,0:T(8,128)(2,1)S(1)}, bf16[512,512]{1,0:T(8,128)(2,1)}, u32[]{:S(2)}) copy-start(bf16[512,512]{1,0:T(8,128)(2,1)} %g_ref.1) | copy-start | bytes 1572868
  3.4 26.8 %copy-start.18 = (f32[512]{0:T(512)S(1)}, f32[512]{0:T(512)}, u32[]{:S(2)}) copy-start(f32[512]{0:T(512)} %param.10) | copy-start | bytes 6148
  25.6 14.4 %all-to-all-start.1 = ((f32[16,32,128]{2,1,0:T(8,128)}), f32[16,32,128]{2,1,0:T(8,128)S(1)}, u32[]{:S(2)}, u32[]{:S(2)}) async-start(f32[16,32,128]{2,1,0:T(8,128)} %state_scan.2), calls=%async_computation.1 | async-start | bytes 524288 | tf_op jit(solution)/shard_map/all_to_all | solution.py:220
  31.7 1.3 %copy-start.5 = (bf16[4,512,512]{2,1,0:T(8,128)(2,1)}, bf16[4,512,512]{2,1,0:T(8,128)(2,1)S(1)}, u32[]{:S(2)}) copy-start(bf16[4,512,512]{2,1,0:T(8,128)(2,1)S(1)} %get-tuple-element.32.scores_ref) | copy-start | bytes 6291460
  33.0 1.0 %copy-start.9 = (f32[512,512]{1,0:T(8,128)}, f32[512,512]{1,0:T(8,128)S(1)}, u32[]{:S(2)}) copy-start(f32[512,512]{1,0:T(8,128)S(1)} %get-tuple-element.25.intra_ref) | copy-start | bytes 3145732
  34.0 0.8 copy-start.14
  34.8 0.8 copy-start.16
  40.0 1.2 %copy-start.10 = (f32[512,512]{1,0:T(8,128)S(1)}, f32[512,512]{1,0:T(8,128)}, u32[]{:S(2)}) copy-start(f32[512,512]{1,0:T(8,128)} %copy-done.9) | copy-start | bytes 3145732
  41.2 1.0 %copy-start.17 = (bf16[512,512]{1,0:T(8,128)(2,1)S(1)}, bf16[512,512]{1,0:T(8,128)(2,1)}, u32[]{:S(2)}) copy-start(bf16[512,512]{1,0:T(8,128)(2,1)} %copy-done.16) | copy-start | bytes 1572868
  42.2 10.0 %copy-start.15 = (bf16[4,128,512]{2,1,0:T(8,128)(2,1)S(1)}, bf16[4,128,512]{2,1,0:T(8,128)(2,1)}, u32[]{:S(2)}) copy-start(bf16[4,128,512]{2,1,0:T(8,128)(2,1)} %copy-done.14) | copy-start | bytes 1572868
  52.8 0.8 copy-start.12
  68.5 14.4 %all-to-all-start.4 = ((f32[16,32,128]{2,1,0:T(8,128)}), f32[16,32,128]{2,1,0:T(8,128)S(1)}, u32[]{:S(2)}, u32[]{:S(2)}) async-start(f32[16,32,128]{2,1,0:T(8,128)} %state_scan.3), calls=%async_computation.4 | async-start | bytes 524288 | tf_op jit(solution)/shard_map/all_to_all | solution.py:220
  73.0 1.6 %copy-start.6 = (bf16[4,512,512]{2,1,0:T(8,128)(2,1)S(1)}, bf16[4,512,512]{2,1,0:T(8,128)(2,1)}, u32[]{:S(2)}) copy-start(bf16[4,512,512]{2,1,0:T(8,128)(2,1)} %copy-done.5) | copy-start | bytes 6291460
  74.6 1.0 %copy-start.13 = (bf16[512,512]{1,0:T(8,128)(2,1)S(1)}, bf16[512,512]{1,0:T(8,128)(2,1)}, u32[]{:S(2)}) copy-start(bf16[512,512]{1,0:T(8,128)(2,1)} %copy-done.12) | copy-start | bytes 1572868
  78.9 1.0 %copy-start.7 = (f32[512,512]{1,0:T(8,128)}, f32[512,512]{1,0:T(8,128)S(1)}, u32[]{:S(2)}) copy-start(f32[512,512]{1,0:T(8,128)S(1)} %get-tuple-element.35.dv_ref) | copy-start | bytes 3145732
  82.8 1.2 %copy-start.8 = (f32[512,512]{1,0:T(8,128)S(1)}, f32[512,512]{1,0:T(8,128)}, u32[]{:S(2)}) copy-start(f32[512,512]{1,0:T(8,128)} %copy-done.7) | copy-start | bytes 3145732

commit v2 on v1

v2 whole, which is shorter than its diff:
```python
import functools

import jax
import jax.numpy as jnp
from jax import lax
from jax.experimental import pallas as pl
from jax.experimental.pallas import tpu as pltpu
from jax.sharding import PartitionSpec as P

DH = 128
WIDTH = 4096
EPSILON = 1e-06
QUARTERS = 4
LOADS = 4

F32 = jnp.float32
BF16 = jnp.bfloat16
I32 = jnp.int32


def dot(a, b, contract):
    return lax.dot_general(a, b, ((contract[:1], contract[1:]), ((), ())), preferred_element_type=F32)


def heads_of(array):
    return [slice(h * DH, (h + 1) * DH) for h in range(array.shape[-1] // DH)]


def row_index(rows):
    return lax.broadcasted_iota(I32, (rows, DH), 0)


def kv_kernel(per, starts_hbm, k_hbm, v_hbm, state_ref, bounds_ref, edges_ref, flags_ref, starts, k_buf, v_buf, sems):
    rows, width = k_buf.shape
    step = rows // LOADS
    starts_copy = pltpu.make_async_copy(starts_hbm, starts, sems.at[0])
    starts_copy.start()
    loads = []
    for i in range(LOADS):
        part = pl.ds(i * step, step)
        loads.append(pltpu.make_async_copy(k_hbm.at[part], k_buf.at[part], sems.at[1 + 2 * i]))
        loads.append(pltpu.make_async_copy(v_hbm.at[part], v_buf.at[part], sems.at[2 + 2 * i]))
    for load in loads:
        load.start()
    pos = lax.axis_index("seq")
    first = pos * rows
    block = (pos // per) * per * rows + rows * lax.broadcasted_iota(I32, (per, DH), 0)
    column = lax.broadcasted_iota(I32, (4, rows), 1)
    head_end = jnp.int32(rows)
    tail = jnp.int32(0)
    begins = jnp.full((4, rows), 0, I32)
    ends = jnp.full((4, rows), rows, I32)
    yes = jnp.ones((per, DH), F32)
    no = jnp.zeros((per, DH), F32)
    keep_forward, take_forward, keep_backward, take_backward = yes, yes, yes, yes
    starts_copy.wait()
    for i in range(starts_hbm.shape[0]):
        start = starts[i]
        here = start - first
        head_end = jnp.where(here > 0, jnp.minimum(head_end, here), head_end)
        tail = jnp.where(here < rows, jnp.maximum(tail, here), tail)
        begins = jnp.where(column >= here, jnp.maximum(begins, here), begins)
        ends = jnp.where(column < here, jnp.minimum(ends, here), ends)
        offset = start - block
        inside = (offset > 0) & (offset < rows)
        keep_forward = jnp.where(inside | (offset == rows), no, keep_forward)
        take_forward = jnp.where(offset == rows, no, take_forward)
        keep_backward = jnp.where(inside | (offset == 0), no, keep_backward)
        take_backward = jnp.where(offset == 0, no, take_backward)
    bounds_ref[0:4] = jnp.full((4, DH), head_end, I32)
    bounds_ref[4:8] = jnp.full((4, DH), tail, I32)
    edges_ref[0:4] = begins
    edges_ref[4:8] = ends
    for i, flag in enumerate((keep_forward, take_forward, keep_backward, take_backward)):
        flags_ref[i] = flag
    for i in range(LOADS):
        loads[2 * i].wait()
        loads[2 * i + 1].wait()
        part = slice(i * step, (i + 1) * step)
        chosen = row_index(step) + i * step >= tail
        for h, cols in enumerate(heads_of(k_buf)):
            k = jnp.where(chosen, k_buf[part, cols], jnp.zeros((), BF16))
            term = dot(k, v_buf[part, cols], (0, 0))
            state_ref[h] = term if i == 0 else state_ref[h] + term


def scan_kernel(backward, flags_ref, x_ref, out_ref):
    count = x_ref.shape[0]
    order = list(range(count))[:: -1 if backward else 1]
    keep, take = (2, 3) if backward else (0, 1)
    running = jnp.zeros(x_ref.shape[1:], F32)
    out_ref[order[0]] = running
    for b, later in zip(order[:-1], order[1:]):
        running = running * flags_ref[keep, b : b + 1] + x_ref[b] * flags_ref[take, b : b + 1]
        out_ref[later] = running


def masked_scores(q, k, ends):
    half = q.shape[0] // 2
    parts = []
    for start, size in ((0, half), (half, 2 * half)):
        token = lax.broadcasted_iota(I32, (half, size), 0) + start
        source = lax.broadcasted_iota(I32, (half, size), 1)
        allowed = (source <= token) & (token < ends[:, :size])
        parts.append(jnp.where(allowed, dot(q[start : start + half], k[:size], (1, 1)), 0.0).astype(BF16))
    return parts


def masked_turned(k, q, begins):
    half = q.shape[0] // 2
    parts = []
    for start, size in ((0, half), (half, 2 * half)):
        token = lax.broadcasted_iota(I32, (size, half), 1) + start
        source = lax.broadcasted_iota(I32, (size, half), 0)
        allowed = (source <= token) & (source >= begins[:, start : start + half])
        parts.append(jnp.where(allowed, dot(k[:size], q[start : start + half], (1, 1)), 0.0).astype(BF16))
    return parts


def intra_kernel(bounds_ref, edges_ref, flags_ref, q_ref, k_ref, v_ref, gain_ref, intra_ref, bounds_out_ref, flags_out_ref, gain_out_ref):
    half = q_ref.shape[0] // 2
    ends = edges_ref[4:5]
    bounds_out_ref[...] = bounds_ref[...]
    flags_out_ref[...] = flags_ref[...]
    gain_out_ref[...] = gain_ref[...]
    for cols in heads_of(q_ref):
        early, late = masked_scores(q_ref[:, cols], k_ref[:, cols], ends)
        intra_ref[:half, cols] = dot(early, v_ref[:half, cols], (1, 0))
        intra_ref[half:, cols] = dot(late, v_ref[:, cols], (1, 0))


def attend_kernel(bounds_ref, q_ref, intra_ref, prefix_ref, g_ref, gain_ref, attended_ref, sums_ref):
    rows = q_ref.shape[0]
    parts = rows // DH
    prefix = [prefix_ref[h].astype(BF16) for h in range(prefix_ref.shape[0])]
    for i in range(parts):
        part = slice(i * DH, (i + 1) * DH)
        from_head = row_index(DH) + i * DH < bounds_ref[0:1]
        squares = jnp.zeros((DH, DH), F32)
        crosses = jnp.zeros((DH, DH), F32)
        for h, cols in enumerate(heads_of(q_ref)):
            carried = dot(q_ref[part, cols], prefix[h], (1, 0))
            attended = intra_ref[part, cols] + jnp.where(from_head, carried, 0.0)
            attended_ref[part, cols] = attended
            squares += attended * attended
            crosses += attended * (gain_ref[:, cols] * g_ref[part, cols].astype(F32))
        square = jnp.sum(squares.T, axis=0, keepdims=True)
        cross = jnp.sum(crosses.T, axis=0, keepdims=True)
        for to in range(sums_ref.shape[0]):
            sums_ref[to, i : i + 1] = square
            sums_ref[to, parts + i : parts + i + 1] = cross


def grad_kernel(bounds_ref, q_ref, attended_ref, g_ref, gain_ref, sums_ref, normed_ref, state_ref):
    rows = attended_ref.shape[0]
    parts = rows // DH
    sums = jnp.sum(sums_ref[...], axis=0)
    inverse = lax.rsqrt(sums[:parts] / WIDTH + EPSILON)
    factor = inverse * inverse * inverse * (sums[parts:] / WIDTH)
    for i in range(parts):
        part = slice(i * DH, (i + 1) * DH)
        from_head = row_index(DH) + i * DH < bounds_ref[0:1]
        inverse_here = jnp.broadcast_to(inverse[i : i + 1], (DH, DH)).T
        factor_here = jnp.broadcast_to(factor[i : i + 1], (DH, DH)).T
        for h, cols in enumerate(heads_of(q_ref)):
            scaled = gain_ref[:, cols] * g_ref[part, cols].astype(F32)
            normed = (scaled * inverse_here - attended_ref[part, cols] * factor_here).astype(BF16)
            normed_ref[part, cols] = normed
            term = dot(jnp.where(from_head, q_ref[part, cols], jnp.zeros((), BF16)), normed, (0, 0))
            state_ref[h] = term if i == 0 else state_ref[h] + term


def products_kernel(
    bounds_ref, edges_ref, q_ref, k_ref, v_ref, normed_ref, prefix_ref, dq_ref, dk_ref, dv_ref
):
    rows = q_ref.shape[0]
    half = rows // 2
    from_head = row_index(rows) < bounds_ref[0:1]
    begins = edges_ref[0:1]
    for h, cols in enumerate(heads_of(q_ref)):
        q, k, normed = q_ref[:, cols], k_ref[:, cols], normed_ref[:, cols]
        early, late = masked_turned(k, q, begins)
        upper = dot(late, normed[half:], (1, 0))
        dv_ref[:half, cols] = (upper[:half] + dot(early, normed[:half], (1, 0))).astype(BF16)
        dv_ref[half:, cols] = upper[half:].astype(BF16)
        early, late = masked_turned(v_ref[:, cols], normed, begins)
        upper = dot(late, q[half:], (1, 0))
        dk_ref[:half, cols] = (upper[:half] + dot(early, q[:half], (1, 0))).astype(BF16)
        dk_ref[half:, cols] = upper[half:].astype(BF16)
        carried = dot(normed, prefix_ref[h].astype(BF16), (1, 1))
        carried = jnp.where(from_head, carried, 0.0)
        dq_ref[:half, cols] = (dot(early, k[:half], (0, 0)) + carried[:half]).astype(BF16)
        dq_ref[half:, cols] = (dot(late, k, (0, 0)) + carried[half:]).astype(BF16)


def final_kernel(bounds_ref, k_ref, v_ref, dk_ref, dv_ref, later_ref, key_hbm, value_hbm, key_buf, value_buf, sems):
    rows = k_ref.shape[0]
    to_tail = row_index(rows) >= bounds_ref[4:5]
    stores = []
    for h, cols in enumerate(heads_of(k_ref)):
        later = later_ref[h].astype(BF16)
        dk = dot(v_ref[:, cols], later, (1, 1))
        key_buf[:, cols] = (dk_ref[:, cols] + jnp.where(to_tail, dk, 0.0)).astype(BF16)
        stores.append(pltpu.make_async_copy(key_buf.at[:, cols], key_hbm.at[:, cols], sems.at[2 * h]))
        stores[-1].start()
        dv = dot(k_ref[:, cols], later, (1, 0))
        value_buf[:, cols] = (dv_ref[:, cols] + jnp.where(to_tail, dv, 0.0)).astype(BF16)
        stores.append(pltpu.make_async_copy(value_buf.at[:, cols], value_hbm.at[:, cols], sems.at[2 * h + 1]))
        stores[-1].start()
    for store in stores:
        store.wait()


HBM = pl.BlockSpec(memory_space=pltpu.HBM)
VMEM = pl.BlockSpec(memory_space=pltpu.VMEM)


def call(kernel, arrays, outs, flops, name, in_specs=None, out_specs=None, scratch=(), room=16):
    out_shape = tuple(jax.ShapeDtypeStruct(s, d) for s, d in outs)
    moved = sum(a.size * a.dtype.itemsize for a in arrays) + sum(o.size * o.dtype.itemsize for o in out_shape)
    return pl.pallas_call(
        kernel,
        out_shape=out_shape,
        in_specs=in_specs or [VMEM] * len(arrays),
        out_specs=out_specs or (VMEM,) * len(outs),
        scratch_shapes=list(scratch),
        compiler_params=pltpu.CompilerParams(vmem_limit_bytes=int(room * 1024 * 1024)),
        cost_estimate=pl.CostEstimate(flops=flops, bytes_accessed=moved, transcendentals=0),
        name=name,
    )(*arrays)


def on_device(queries, keys, values, out_grad, gain, doc_starts):
    rows, width = queries.shape
    heads = width // DH
    per = lax.axis_size("seq") // QUARTERS
    head_devices = lax.axis_size("head")
    gain_row = gain.reshape(1, width)
    groups = [[g * per + i for i in range(per)] for g in range(QUARTERS)]
    state_shape = (heads, DH, DH)
    pieces = (per, heads * DH // per, DH)
    state_flops = 2 * rows * width * DH
    full_flops = 2 * rows * rows * width
    whole = (rows, width)

    def swap(x):
        return lax.all_to_all(x.reshape(pieces), "seq", 0, 0, axis_index_groups=groups, tiled=True)

    def scan(state, flags, backward):
        (mine,) = call(functools.partial(scan_kernel, backward), (flags, swap(state)), [(pieces, F32)], 0, "state_scan")
        return swap(mine).reshape(state_shape)

    kv_state, bounds, edges, flags = call(
        functools.partial(kv_kernel, per),
        (doc_starts, keys, values),
        [(state_shape, F32), ((8, DH), I32), ((8, rows), I32), ((4, per, DH), F32)],
        state_flops,
        "kv_state",
        in_specs=[HBM] * 3,
        room=60,
        scratch=[
            pltpu.SMEM(doc_starts.shape, I32),
            pltpu.VMEM(whole, BF16),
            pltpu.VMEM(whole, BF16),
            pltpu.SemaphoreType.DMA((1 + 2 * LOADS,)),
        ],
    )
    intra, bounds, flags, gain_row = call(
        intra_kernel,
        (bounds, edges, flags, queries, keys, values, gain_row),
        [(whole, F32), (bounds.shape, I32), (flags.shape, F32), (gain_row.shape, F32)],
        2 * full_flops,
        "intra",
    )
    prefix = scan(kv_state, flags, False)
    attended, sums = call(
        attend_kernel,
        (bounds, queries, intra, prefix, out_grad, gain_row),
        [(whole, F32), ((head_devices, 2 * rows // DH, DH), F32)],
        state_flops,
        "attend",
    )
    sums = lax.all_to_all(sums, "head", 0, 0, tiled=True)
    normed, grad_state = call(
        grad_kernel,
        (bounds, queries, attended, out_grad, gain_row, sums),
        [(whole, BF16), (state_shape, F32)],
        state_flops,
        "normed_grad",
    )
    later = scan(grad_state, flags, True)
    query_grad, key_part, value_part = call(
        products_kernel,
        (bounds, edges, queries, keys, values, normed, prefix),
        [(whole, BF16), (whole, BF16), (whole, BF16)],
        5 * full_flops + state_flops,
        "products",
    )
    key_grad, value_grad = call(
        final_kernel,
        (bounds, keys, values, key_part, value_part, later),
        [(whole, BF16), (whole, BF16)],
        2 * state_flops,
        "key_value_grad",
        out_specs=(HBM, HBM),
        scratch=[
            pltpu.VMEM(whole, BF16),
            pltpu.VMEM(whole, BF16),
            pltpu.SemaphoreType.DMA((2 * heads,)),
        ],
    )
    return query_grad, key_grad, value_grad


def solution(mesh):
    placed = (P("seq", "head"),) * 4 + (P("head"), P())
    return jax.shard_map(
        on_device,
        mesh=mesh,
        in_specs=placed,
        out_specs=(P("seq", "head"),) * 3,
        check_vma=False,
    )
```

time: 86 us -> 79.1 us (0.920)
  local copies, waits for them, and re-layouts: 14.6 us -> 3.19 us
  starting transfers between devices: 9.12 us -> 14.2 us
  blocking collectives: 42.9 us -> 38 us
  waiting for transfers between devices: 7.36 us -> 12.2 us
    unnamed x40 -> x22, local copies, waits for them, and re-layouts: 14.6 us -> 3.19 us
    all_to_all x2, starting transfers between devices: 9.12 us -> 14.2 us  [swap(): lax.all_to_all(x.reshape(pieces), 'seq', 0, 0, axis_index_groups=groups,...]
    all_to_all x2, blocking collectives: 33.4 us -> 28.4 us  [swap(): lax.all_to_all(x.reshape(pieces), 'seq', 0, 0, axis_index_groups=groups,...]
    all_to_all x2, waiting for transfers between devices: 7.36 us -> 12.2 us  [swap(): lax.all_to_all(x.reshape(pieces), 'seq', 0, 0, axis_index_groups=groups,...]
  transfers between devices with their start and end apart: 2 -> 2, of which waited for: 2 -> 2; matrix products, arithmetic and copies ran while one was open for 0% -> 0% of each run, Pallas kernels for 5% -> 6%
where the time goes in v2:
time: 79.1 us; the launch traced here: 78.4 us
  blocking collectives  38 us (48%)
  starting transfers between devices  14.2 us (18%)
  waiting for transfers between devices  12.2 us (15%)
  Pallas kernels  10.1 us (13%)
  local copies, waits for them, and re-layouts  3.19 us (4%)
    all_to_all x2, blocking collectives, swap(): lax.all_to_all(x.reshape(pieces), 'seq', 0, 0, axis_index_groups=groups,...  28.4 us
    all_to_all x2, starting transfers between devices, swap(): lax.all_to_all(x.reshape(pieces), 'seq', 0, 0, axis_index_groups=groups,...  14.2 us
    all_to_all x2, waiting for transfers between devices, swap(): lax.all_to_all(x.reshape(pieces), 'seq', 0, 0, axis_index_groups=groups,...  12.2 us
    pallas_call x8, Pallas kernels, call(): pl.pallas_call(kernel, out_shape=out_shape, in_specs=in_specs or [VMEM] *...  10.1 us
    all_to_all x1, blocking collectives, on_device(): sums = lax.all_to_all(sums, 'head', 0, 0, tiled=True)  9.55 us
    unnamed x22, local copies, waits for them, and re-layouts  3.19 us
  transfers between devices with their start and end apart: 2, of which 2 were waited for; matrix products, arithmetic and copies ran while one was open for 0% of the time, Pallas kernels for 6%

profile of v2, /device:TPU:136, one launch (start us, length us, event | category | flops | bytes accessed | tf_op | source)
XLA Modules:
  0.0 78.4 jit_solution(9977298505874027332)
XLA Ops:
  0.7 2.4 %kv_state.1 = (f32[4,128,128]{2,1,0:T(8,128)}, s32[8,128]{1,0:T(8,128)}, s32[8,512]{1,0:T(8,128)}, f32[4,16,128]{2,1,0:T(8,128)}) custom-call(s32[25]{0:T(128)} %starts_hbm.1, bf16[512,512]{1,0:T(8,128)(2,1)} %k_ref.5, bf16[512,512]{1,0:T(8,128)(2,1)} %v_ref.5), custom_call_target="tpu_custom_call" | custom-call | flops 67108864 | bytes 1364068 | tf_op jit(solution)/shard_map/kv_state/pallas_call | solution.py:221
  3.1 0.0 copy-start.1
  3.1 9.5 %all-to-all-start = ((f32[16,32,128]{2,1,0:T(8,128)}), f32[16,32,128]{2,1,0:T(8,128)S(1)}, u32[]{:S(2)}, u32[]{:S(2)}) async-start(f32[16,32,128]{2,1,0:T(8,128)} %bitcast.10), calls=%async_computation | async-start | bytes 524288 | tf_op jit(solution)/shard_map/all_to_all | solution.py:247
  12.6 0.0 copy-start.10
  12.6 0.0 copy-done.2
  12.6 0.6 copy-done.9
  13.3 0.0 copy-done.10
  13.3 0.8 copy-done.6
  14.0 0.7 copy-done.7
  14.8 1.1 %intra.1 = (f32[512,512]{1,0:T(8,128)S(1)}, s32[8,128]{1,0:T(8,128)S(1)}, f32[4,16,128]{2,1,0:T(8,128)S(1)}, f32[1,512]{1,0:T(1,128)S(1)}) custom-call(s32[8,128]{1,0:T(8,128)S(1)} %copy-done.9, s32[8,512]{1,0:T(8,128)S(1)} %copy-done.7, f32[4,16,128]{2,1,0:T(8,128)S(1)} %copy-done.6, bf16[512,512]{1,0:T(8,128)(2,1)S(1)} %copy-done.1, ...), custom_call_target="tpu_custom_call" | custom-call | flops 536870912 | bytes 2715648 | tf_op jit(solution)/shard_map/intra/pallas_call | solution.py:221
  15.9 6.8 %all-to-all-done.x_ref = f32[16,32,128]{2,1,0:T(8,128)S(1)} async-done(((f32[16,32,128]{2,1,0:T(8,128)}), f32[16,32,128]{2,1,0:T(8,128)S(1)}, u32[]{:S(2)}, u32[]{:S(2)}) %all-to-all-start) | async-done | bytes 262176 | tf_op jit(solution)/shard_map/all_to_all | solution.py:247
  22.7 14.3 %all_to_all.25 = f32[16,32,128]{2,1,0:T(8,128)S(1)} all-to-all(f32[16,32,128]{2,1,0:T(8,128)S(1)} %state_scan.2), channel_id=1, replica_groups={{0,8,16,24,32,40,48,56,64,72,80,88,96,104,112,120},{128,136,144,152,160..., dimensions={0} | all-to-all | bytes 524288 | tf_op jit(solution)/shard_map/all_to_all | solution.py:247
  37.0 0.6 attend.1
  37.6 9.5 %all_to_all.26.sums_ref = f32[8,8,128]{2,1,0:T(8,128)S(1)} all-to-all(f32[8,8,128]{2,1,0:T(8,128)S(1)} %get-tuple-element.29), channel_id=1, replica_groups=mesh['seq'=64,'head'=8] {'head'}, dimensions={0} | all-to-all | bytes 65536 | tf_op jit(solution)/shard_map/all_to_all | solution.py:283
  47.1 0.6 normed_grad.1
  47.7 0.0 copy-start.4
  47.8 14.1 %all_to_all.27.x_ref = f32[16,32,128]{2,1,0:T(8,128)S(1)} all-to-all(f32[16,32,128]{2,1,0:T(8,128)S(1)} %bitcast.8), channel_id=1, replica_groups={{0,8,16,24,32,40,48,56,64,72,80,88,96,104,112,120},{128,136,144,152,160..., dimensions={0} | all-to-all | bytes 524288 | tf_op jit(solution)/shard_map/all_to_all | solution.py:247
  61.9 0.7 state_scan.3
  62.6 4.7 %all-to-all-start.4 = ((f32[16,32,128]{2,1,0:T(8,128)}), f32[16,32,128]{2,1,0:T(8,128)S(1)}, u32[]{:S(2)}, u32[]{:S(2)}) async-start(f32[16,32,128]{2,1,0:T(8,128)} %state_scan.3), calls=%async_computation.4 | async-start | bytes 524288 | tf_op jit(solution)/shard_map/all_to_all | solution.py:247
  67.3 0.0 copy-start.5
  67.3 1.0 %copy-done.5 = bf16[512,512]{1,0:T(8,128)(2,1)S(1)} copy-done((bf16[512,512]{1,0:T(8,128)(2,1)S(1)}, bf16[512,512]{1,0:T(8,128)(2,1)}, u32[]{:S(2)}) %copy-start.5) | copy-done | bytes 524312
  68.4 3.3 %products.1 = (bf16[512,512]{1,0:T(8,128)(2,1)}, bf16[512,512]{1,0:T(8,128)(2,1)S(1)}, bf16[512,512]{1,0:T(8,128)(2,1)S(1)}) custom-call(s32[8,128]{1,0:T(8,128)S(1)} %get-tuple-element.23.bounds_ref, s32[8,512]{1,0:T(8,128)S(1)} %copy-done.8, bf16[512,512]{1,0:T(8,128)(2,1)S(1)} %copy-done.1, bf16[512,512]{1,0:T(8,128)(2,1)S(1)} %copy-done.2, ...), custom_call_target="tpu_custom_call" | custom-call | flops 1409286144 | bytes 3952640 | tf_op jit(solution)/shard_map/products/pallas_call | solution.py:221
  71.7 5.4 %all-to-all-done.4 = f32[16,32,128]{2,1,0:T(8,128)S(1)} async-done(((f32[16,32,128]{2,1,0:T(8,128)}), f32[16,32,128]{2,1,0:T(8,128)S(1)}, u32[]{:S(2)}, u32[]{:S(2)}) %all-to-all-start.4) | async-done | bytes 262176 | tf_op jit(solution)/shard_map/all_to_all | solution.py:247
  77.1 1.3 %key_value_grad.1 = (bf16[512,512]{1,0:T(8,128)(2,1)}, bf16[512,512]{1,0:T(8,128)(2,1)}) custom-call(s32[8,128]{1,0:T(8,128)S(1)} %get-tuple-element.23.bounds_ref, bf16[512,512]{1,0:T(8,128)(2,1)S(1)} %copy-done.2, bf16[512,512]{1,0:T(8,128)(2,1)S(1)} %copy-done.3, bf16[512,512]{1,0:T(8,128)(2,1)S(1)} %get-tuple-element.32.dk_ref, ...), custom_call_target="tpu_custom_call" | custom-call | flops 134217728 | bytes 3411968 | tf_op jit(solution)/shard_map/key_value_grad/pallas_call | solution.py:221
  (13 shorter events, 0.1 us)
Async XLA Ops:
  0.6 12.0 %copy-start.2 = (bf16[512,512]{1,0:T(8,128)(2,1)S(1)}, bf16[512,512]{1,0:T(8,128)(2,1)}, u32[]{:S(2)}) copy-start(bf16[512,512]{1,0:T(8,128)(2,1)} %k_ref.5) | copy-start | bytes 1572868
  0.6 12.0 %copy-start.3 = (bf16[512,512]{1,0:T(8,128)(2,1)S(1)}, bf16[512,512]{1,0:T(8,128)(2,1)}, u32[]{:S(2)}) copy-start(bf16[512,512]{1,0:T(8,128)(2,1)} %v_ref.5) | copy-start | bytes 1572868
  3.1 9.6 %copy-start.1 = (bf16[512,512]{1,0:T(8,128)(2,1)S(1)}, bf16[512,512]{1,0:T(8,128)(2,1)}, u32[]{:S(2)}) copy-start(bf16[512,512]{1,0:T(8,128)(2,1)} %q_ref.7) | copy-start | bytes 1572868
  3.1 19.6 %all-to-all-start = ((f32[16,32,128]{2,1,0:T(8,128)}), f32[16,32,128]{2,1,0:T(8,128)S(1)}, u32[]{:S(2)}, u32[]{:S(2)}) async-start(f32[16,32,128]{2,1,0:T(8,128)} %bitcast.10), calls=%async_computation | async-start | bytes 524288 | tf_op jit(solution)/shard_map/all_to_all | solution.py:247
  12.6 0.7 copy-start.9
  12.6 0.7 copy-start.10
  13.3 0.8 copy-start.6
  14.0 0.7 copy-start.7
  22.7 14.3 %copy-start = (bf16[512,512]{1,0:T(8,128)(2,1)S(1)}, bf16[512,512]{1,0:T(8,128)(2,1)}, u32[]{:S(2)}) copy-start(bf16[512,512]{1,0:T(8,128)(2,1)} %g_ref.3) | copy-start | bytes 1572868
  47.7 14.2 %copy-start.4 = (bf16[512,512]{1,0:T(8,128)(2,1)}, bf16[512,512]{1,0:T(8,128)(2,1)S(1)}, u32[]{:S(2)}) copy-start(bf16[512,512]{1,0:T(8,128)(2,1)S(1)} %get-tuple-element.30.normed_ref) | copy-start | bytes 1572868
  62.6 4.7 %copy-start.8 = (s32[8,512]{1,0:T(8,128)S(1)}, s32[8,512]{1,0:T(8,128)}, u32[]{:S(2)}) copy-start(s32[8,512]{1,0:T(8,128)} %get-tuple-element.21.edges_ref) | copy-start | bytes 49156
  62.6 14.5 %all-to-all-start.4 = ((f32[16,32,128]{2,1,0:T(8,128)}), f32[16,32,128]{2,1,0:T(8,128)S(1)}, u32[]{:S(2)}, u32[]{:S(2)}) async-start(f32[16,32,128]{2,1,0:T(8,128)} %state_scan.3), calls=%async_computation.4 | async-start | bytes 524288 | tf_op jit(solution)/shard_map/all_to_all | solution.py:247
  67.3 1.0 %copy-start.5 = (bf16[512,512]{1,0:T(8,128)(2,1)S(1)}, bf16[512,512]{1,0:T(8,128)(2,1)}, u32[]{:S(2)}) copy-start(bf16[512,512]{1,0:T(8,128)(2,1)} %copy-done.4) | copy-start | bytes 1572868

commit v3 on v2

--- a/solution.py
+++ b/solution.py
@@ -84,15 +84,24 @@
             state_ref[h] = term if i == 0 else state_ref[h] + term
 
 
+def fold_order(per):
+    row = per // 2
+    ring = [i // 2 if i % 2 == 0 else row - 1 - i // 2 for i in range(row)]
+    return [z * row + y for z in range(2) for y in ring]
+
+
 def scan_kernel(backward, flags_ref, x_ref, out_ref):
     count = x_ref.shape[0]
     order = list(range(count))[:: -1 if backward else 1]
+    folded = fold_order(count)
+    odd = lax.rem(lax.axis_index("head"), 2) == 1
+    place = [jnp.where(odd, folded.index(b), b) for b in range(count)]
     keep, take = (2, 3) if backward else (0, 1)
     running = jnp.zeros(x_ref.shape[1:], F32)
-    out_ref[order[0]] = running
+    out_ref[place[order[0]]] = running
     for b, later in zip(order[:-1], order[1:]):
-        running = running * flags_ref[keep, b : b + 1] + x_ref[b] * flags_ref[take, b : b + 1]
-        out_ref[later] = running
+        running = running * flags_ref[keep, b : b + 1] + x_ref[place[b]] * flags_ref[take, b : b + 1]
+        out_ref[place[later]] = running
 
 
 def masked_scores(q, k, ends):
@@ -236,7 +245,10 @@
     per = lax.axis_size("seq") // QUARTERS
     head_devices = lax.axis_size("head")
     gain_row = gain.reshape(1, width)
-    groups = [[g * per + i for i in range(per)] for g in range(QUARTERS)]
+    orders = (list(range(per)), fold_order(per))
+    groups = [
+        [(g * per + b) * head_devices + m for b in orders[m % 2]] for g in range(QUARTERS) for m in range(head_devices)
+    ]
     state_shape = (heads, DH, DH)
     pieces = (per, heads * DH // per, DH)
     state_flops = 2 * rows * width * DH
@@ -244,7 +256,7 @@
     whole = (rows, width)
 
     def swap(x):
-        return lax.all_to_all(x.reshape(pieces), "seq", 0, 0, axis_index_groups=groups, tiled=True)
+        return lax.all_to_all(x.reshape(pieces), ("seq", "head"), 0, 0, axis_index_groups=groups, tiled=True)
 
     def scan(state, flags, backward):
         (mine,) = call(functools.partial(scan_kernel, backward), (flags, swap(state)), [(pieces, F32)], 0, "state_scan")

time: 79.1 us -> 78.2 us (0.989)
  the two profiles are of different devices: /device:TPU:136 before, /device:TPU:128 now
where the time goes in v3:
time: 78.2 us; the launch traced here: 77.5 us
  blocking collectives  37.6 us (48%)
  starting transfers between devices  13.8 us (18%)
  waiting for transfers between devices  12.1 us (15%)
  Pallas kernels  10.1 us (13%)
  local copies, waits for them, and re-layouts  3.19 us (4%)
    all_to_all x2, blocking collectives, swap(): lax.all_to_all(x.reshape(pieces), ('seq', 'head'), 0, 0, axis_index_group...  28 us
    all_to_all x2, starting transfers between devices, swap(): lax.all_to_all(x.reshape(pieces), ('seq', 'head'), 0, 0, axis_index_group...  13.8 us
    all_to_all x2, waiting for transfers between devices, swap(): lax.all_to_all(x.reshape(pieces), ('seq', 'head'), 0, 0, axis_index_group...  12.1 us
    pallas_call x8, Pallas kernels, call(): pl.pallas_call(kernel, out_shape=out_shape, in_specs=in_specs or [VMEM] *...  10.1 us
    all_to_all x1, blocking collectives, on_device(): sums = lax.all_to_all(sums, 'head', 0, 0, tiled=True)  9.55 us
    unnamed x22, local copies, waits for them, and re-layouts  3.19 us
  transfers between devices with their start and end apart: 2, of which 2 were waited for; matrix products, arithmetic and copies ran while one was open for 0% of the time, Pallas kernels for 6%

profile of v3, /device:TPU:128, one launch (start us, length us, event | category | flops | bytes accessed | tf_op | source)
XLA Modules:
  0.0 77.5 jit_solution(10781820498400159897)
XLA Ops:
  0.7 2.4 %kv_state.1 = (f32[4,128,128]{2,1,0:T(8,128)}, s32[8,128]{1,0:T(8,128)}, s32[8,512]{1,0:T(8,128)}, f32[4,16,128]{2,1,0:T(8,128)}) custom-call(s32[25]{0:T(128)} %starts_hbm.1, bf16[512,512]{1,0:T(8,128)(2,1)} %k_ref.5, bf16[512,512]{1,0:T(8,128)(2,1)} %v_ref.5), custom_call_target="tpu_custom_call" | custom-call | flops 67108864 | bytes 1364068 | tf_op jit(solution)/shard_map/kv_state/pallas_call | solution.py:230
  3.1 0.0 copy-start.1
  3.1 9.2 %all-to-all-start = ((f32[16,32,128]{2,1,0:T(8,128)}), f32[16,32,128]{2,1,0:T(8,128)S(1)}, u32[]{:S(2)}, u32[]{:S(2)}) async-start(f32[16,32,128]{2,1,0:T(8,128)} %bitcast.10), calls=%async_computation | async-start | bytes 524288 | tf_op jit(solution)/shard_map/all_to_all | solution.py:259
  12.2 0.0 copy-start.9
  12.3 0.0 copy-start.10
  12.3 0.6 copy-done.9
  12.9 0.0 copy-done.10
  12.9 0.8 copy-done.6
  13.7 0.7 copy-done.7
  14.4 1.1 %intra.1 = (f32[512,512]{1,0:T(8,128)S(1)}, s32[8,128]{1,0:T(8,128)S(1)}, f32[4,16,128]{2,1,0:T(8,128)S(1)}, f32[1,512]{1,0:T(1,128)S(1)}) custom-call(s32[8,128]{1,0:T(8,128)S(1)} %copy-done.9, s32[8,512]{1,0:T(8,128)S(1)} %copy-done.7, f32[4,16,128]{2,1,0:T(8,128)S(1)} %copy-done.6, bf16[512,512]{1,0:T(8,128)(2,1)S(1)} %copy-done.1, ...), custom_call_target="tpu_custom_call" | custom-call | flops 536870912 | bytes 2715648 | tf_op jit(solution)/shard_map/intra/pallas_call | solution.py:230
  15.5 6.8 %all-to-all-done.x_ref = f32[16,32,128]{2,1,0:T(8,128)S(1)} async-done(((f32[16,32,128]{2,1,0:T(8,128)}), f32[16,32,128]{2,1,0:T(8,128)S(1)}, u32[]{:S(2)}, u32[]{:S(2)}) %all-to-all-start) | async-done | bytes 262176 | tf_op jit(solution)/shard_map/all_to_all | solution.py:259
  22.3 14.3 %all_to_all.25 = f32[16,32,128]{2,1,0:T(8,128)S(1)} all-to-all(f32[16,32,128]{2,1,0:T(8,128)S(1)} %state_scan.2), channel_id=1, replica_groups={{0,8,16,24,32,40,48,56,64,72,80,88,96,104,112,120},{1,57,9,49,17,41,25,..., dimensions={0} | all-to-all | bytes 524288 | tf_op jit(solution)/shard_map/all_to_all | solution.py:259
  36.6 0.6 attend.1
  37.1 9.5 %all_to_all.26.sums_ref = f32[8,8,128]{2,1,0:T(8,128)S(1)} all-to-all(f32[8,8,128]{2,1,0:T(8,128)S(1)} %get-tuple-element.29), channel_id=1, replica_groups=mesh['seq'=64,'head'=8] {'head'}, dimensions={0} | all-to-all | bytes 65536 | tf_op jit(solution)/shard_map/all_to_all | solution.py:295
  46.7 0.6 normed_grad.1
  47.3 0.0 copy-start.4
  47.3 13.7 %all_to_all.27.x_ref = f32[16,32,128]{2,1,0:T(8,128)S(1)} all-to-all(f32[16,32,128]{2,1,0:T(8,128)S(1)} %bitcast.8), channel_id=1, replica_groups={{0,8,16,24,32,40,48,56,64,72,80,88,96,104,112,120},{1,57,9,49,17,41,25,..., dimensions={0} | all-to-all | bytes 524288 | tf_op jit(solution)/shard_map/all_to_all | solution.py:259
  61.1 0.7 state_scan.3
  61.8 4.7 %all-to-all-start.4 = ((f32[16,32,128]{2,1,0:T(8,128)}), f32[16,32,128]{2,1,0:T(8,128)S(1)}, u32[]{:S(2)}, u32[]{:S(2)}) async-start(f32[16,32,128]{2,1,0:T(8,128)} %state_scan.3), calls=%async_computation.4 | async-start | bytes 524288 | tf_op jit(solution)/shard_map/all_to_all | solution.py:259
  66.5 0.0 copy-start.5
  66.5 1.0 %copy-done.5 = bf16[512,512]{1,0:T(8,128)(2,1)S(1)} copy-done((bf16[512,512]{1,0:T(8,128)(2,1)S(1)}, bf16[512,512]{1,0:T(8,128)(2,1)}, u32[]{:S(2)}) %copy-start.5) | copy-done | bytes 524312
  67.5 3.3 %products.1 = (bf16[512,512]{1,0:T(8,128)(2,1)}, bf16[512,512]{1,0:T(8,128)(2,1)S(1)}, bf16[512,512]{1,0:T(8,128)(2,1)S(1)}) custom-call(s32[8,128]{1,0:T(8,128)S(1)} %get-tuple-element.23.bounds_ref, s32[8,512]{1,0:T(8,128)S(1)} %copy-done.8, bf16[512,512]{1,0:T(8,128)(2,1)S(1)} %copy-done.1, bf16[512,512]{1,0:T(8,128)(2,1)S(1)} %copy-done.2, ...), custom_call_target="tpu_custom_call" | custom-call | flops 1409286144 | bytes 3952640 | tf_op jit(solution)/shard_map/products/pallas_call | solution.py:230
  70.9 5.3 %all-to-all-done.4 = f32[16,32,128]{2,1,0:T(8,128)S(1)} async-done(((f32[16,32,128]{2,1,0:T(8,128)}), f32[16,32,128]{2,1,0:T(8,128)S(1)}, u32[]{:S(2)}, u32[]{:S(2)}) %all-to-all-start.4) | async-done | bytes 262176 | tf_op jit(solution)/shard_map/all_to_all | solution.py:259
  76.2 1.3 %key_value_grad.1 = (bf16[512,512]{1,0:T(8,128)(2,1)}, bf16[512,512]{1,0:T(8,128)(2,1)}) custom-call(s32[8,128]{1,0:T(8,128)S(1)} %get-tuple-element.23.bounds_ref, bf16[512,512]{1,0:T(8,128)(2,1)S(1)} %copy-done.2, bf16[512,512]{1,0:T(8,128)(2,1)S(1)} %copy-done.3, bf16[512,512]{1,0:T(8,128)(2,1)S(1)} %get-tuple-element.32.dk_ref, ...), custom_call_target="tpu_custom_call" | custom-call | flops 134217728 | bytes 3411968 | tf_op jit(solution)/shard_map/key_value_grad/pallas_call | solution.py:230
  (13 shorter events, 0.1 us)
Async XLA Ops:
  0.6 11.6 %copy-start.2 = (bf16[512,512]{1,0:T(8,128)(2,1)S(1)}, bf16[512,512]{1,0:T(8,128)(2,1)}, u32[]{:S(2)}) copy-start(bf16[512,512]{1,0:T(8,128)(2,1)} %k_ref.5) | copy-start | bytes 1572868
  0.6 11.6 %copy-start.3 = (bf16[512,512]{1,0:T(8,128)(2,1)S(1)}, bf16[512,512]{1,0:T(8,128)(2,1)}, u32[]{:S(2)}) copy-start(bf16[512,512]{1,0:T(8,128)(2,1)} %v_ref.5) | copy-start | bytes 1572868
  3.1 9.2 %copy-start.1 = (bf16[512,512]{1,0:T(8,128)(2,1)S(1)}, bf16[512,512]{1,0:T(8,128)(2,1)}, u32[]{:S(2)}) copy-start(bf16[512,512]{1,0:T(8,128)(2,1)} %q_ref.7) | copy-start | bytes 1572868
  3.1 19.2 %all-to-all-start = ((f32[16,32,128]{2,1,0:T(8,128)}), f32[16,32,128]{2,1,0:T(8,128)S(1)}, u32[]{:S(2)}, u32[]{:S(2)}) async-start(f32[16,32,128]{2,1,0:T(8,128)} %bitcast.10), calls=%async_computation | async-start | bytes 524288 | tf_op jit(solution)/shard_map/all_to_all | solution.py:259
  12.2 0.7 copy-start.9
  12.3 0.7 copy-start.10
  12.9 0.8 copy-start.6
  13.7 0.7 copy-start.7
  22.3 14.3 %copy-start = (bf16[512,512]{1,0:T(8,128)(2,1)S(1)}, bf16[512,512]{1,0:T(8,128)(2,1)}, u32[]{:S(2)}) copy-start(bf16[512,512]{1,0:T(8,128)(2,1)} %g_ref.3) | copy-start | bytes 1572868
  47.3 13.8 %copy-start.4 = (bf16[512,512]{1,0:T(8,128)(2,1)}, bf16[512,512]{1,0:T(8,128)(2,1)S(1)}, u32[]{:S(2)}) copy-start(bf16[512,512]{1,0:T(8,128)(2,1)S(1)} %get-tuple-element.30.normed_ref) | copy-start | bytes 1572868
  61.8 4.7 %copy-start.8 = (s32[8,512]{1,0:T(8,128)S(1)}, s32[8,512]{1,0:T(8,128)}, u32[]{:S(2)}) copy-start(s32[8,512]{1,0:T(8,128)} %get-tuple-element.21.edges_ref) | copy-start | bytes 49156
  61.8 14.4 %all-to-all-start.4 = ((f32[16,32,128]{2,1,0:T(8,128)}), f32[16,32,128]{2,1,0:T(8,128)S(1)}, u32[]{:S(2)}, u32[]{:S(2)}) async-start(f32[16,32,128]{2,1,0:T(8,128)} %state_scan.3), calls=%async_computation.4 | async-start | bytes 524288 | tf_op jit(solution)/shard_map/all_to_all | solution.py:259
  66.5 1.0 %copy-start.5 = (bf16[512,512]{1,0:T(8,128)(2,1)S(1)}, bf16[512,512]{1,0:T(8,128)(2,1)}, u32[]{:S(2)}) copy-start(bf16[512,512]{1,0:T(8,128)(2,1)} %copy-done.4) | copy-start | bytes 1572868

commit v4 on v3

--- a/solution.py
+++ b/solution.py
@@ -84,18 +84,20 @@
             state_ref[h] = term if i == 0 else state_ref[h] + term
 
 
-def fold_order(per):
-    row = per // 2
-    ring = [i // 2 if i % 2 == 0 else row - 1 - i // 2 for i in range(row)]
-    return [z * row + y for z in range(2) for y in ring]
+def block_orders(per, backward):
+    ring = per // 2
+    plain = list(range(per))
+    fold = [i // 2 if i % 2 == 0 else ring - 1 - i // 2 for i in range(ring)]
+    folded = [z * ring + y for z in range(2) for y in fold]
+    return plain, folded if backward else folded[ring:] + folded[:ring]
 
 
 def scan_kernel(backward, flags_ref, x_ref, out_ref):
     count = x_ref.shape[0]
     order = list(range(count))[:: -1 if backward else 1]
-    folded = fold_order(count)
+    even_order, odd_order = block_orders(count, backward)
     odd = lax.rem(lax.axis_index("head"), 2) == 1
-    place = [jnp.where(odd, folded.index(b), b) for b in range(count)]
+    place = [jnp.where(odd, odd_order.index(b), even_order.index(b)) for b in range(count)]
     keep, take = (2, 3) if backward else (0, 1)
     running = jnp.zeros(x_ref.shape[1:], F32)
     out_ref[place[order[0]]] = running
@@ -245,22 +247,25 @@
     per = lax.axis_size("seq") // QUARTERS
     head_devices = lax.axis_size("head")
     gain_row = gain.reshape(1, width)
-    orders = (list(range(per)), fold_order(per))
-    groups = [
-        [(g * per + b) * head_devices + m for b in orders[m % 2]] for g in range(QUARTERS) for m in range(head_devices)
-    ]
+    all_groups = []
+    for backward in (False, True):
+        orders = block_orders(per, backward)
+        all_groups.append(
+            [[(g * per + b) * head_devices + m for b in orders[m % 2]] for g in range(QUARTERS) for m in range(head_devices)]
+        )
     state_shape = (heads, DH, DH)
     pieces = (per, heads * DH // per, DH)
     state_flops = 2 * rows * width * DH
     full_flops = 2 * rows * rows * width
     whole = (rows, width)
 
-    def swap(x):
+    def swap(x, backward):
+        groups = all_groups[backward]
         return lax.all_to_all(x.reshape(pieces), ("seq", "head"), 0, 0, axis_index_groups=groups, tiled=True)
 
     def scan(state, flags, backward):
-        (mine,) = call(functools.partial(scan_kernel, backward), (flags, swap(state)), [(pieces, F32)], 0, "state_scan")
-        return swap(mine).reshape(state_shape)
+        (mine,) = call(functools.partial(scan_kernel, backward), (flags, swap(state, backward)), [(pieces, F32)], 0, "state_scan")
+        return swap(mine, backward).reshape(state_shape)
 
     kv_state, bounds, edges, flags = call(
         functools.partial(kv_kernel, per),

time: 78.2 us -> 77.9 us (level)
  no operation moved by 1% of the time
where the time goes in v4:
time: 77.9 us; the launch traced here: 77.3 us
  blocking collectives  37.4 us (48%)
  starting transfers between devices  13.8 us (18%)
  waiting for transfers between devices  11.9 us (15%)
  Pallas kernels  10.1 us (13%)
  local copies, waits for them, and re-layouts  3.19 us (4%)
    all_to_all x2, blocking collectives, swap(): lax.all_to_all(x.reshape(pieces), ('seq', 'head'), 0, 0, axis_index_group...  27.9 us
    all_to_all x2, starting transfers between devices, swap(): lax.all_to_all(x.reshape(pieces), ('seq', 'head'), 0, 0, axis_index_group...  13.8 us
    all_to_all x2, waiting for transfers between devices, swap(): lax.all_to_all(x.reshape(pieces), ('seq', 'head'), 0, 0, axis_index_group...  11.9 us
    pallas_call x8, Pallas kernels, call(): pl.pallas_call(kernel, out_shape=out_shape, in_specs=in_specs or [VMEM] *...  10.1 us
    all_to_all x1, blocking collectives, on_device(): sums = lax.all_to_all(sums, 'head', 0, 0, tiled=True)  9.55 us
    unnamed x22, local copies, waits for them, and re-layouts  3.19 us
  transfers between devices with their start and end apart: 2, of which 2 were waited for; matrix products, arithmetic and copies ran while one was open for 0% of the time, Pallas kernels for 6%

profile of v4, /device:TPU:128, one launch (start us, length us, event | category | flops | bytes accessed | tf_op | source)
XLA Modules:
  0.0 77.3 jit_solution(2130061283257192995)
XLA Ops:
  0.7 2.4 %kv_state.1 = (f32[4,128,128]{2,1,0:T(8,128)}, s32[8,128]{1,0:T(8,128)}, s32[8,512]{1,0:T(8,128)}, f32[4,16,128]{2,1,0:T(8,128)}) custom-call(s32[25]{0:T(128)} %starts_hbm.1, bf16[512,512]{1,0:T(8,128)(2,1)} %k_ref.5, bf16[512,512]{1,0:T(8,128)(2,1)} %v_ref.5), custom_call_target="tpu_custom_call" | custom-call | flops 67108864 | bytes 1364068 | tf_op jit(solution)/shard_map/kv_state/pallas_call | solution.py:232
  3.1 0.0 copy-start.1
  3.1 9.2 %all-to-all-start = ((f32[16,32,128]{2,1,0:T(8,128)}), f32[16,32,128]{2,1,0:T(8,128)S(1)}, u32[]{:S(2)}, u32[]{:S(2)}) async-start(f32[16,32,128]{2,1,0:T(8,128)} %bitcast.10), calls=%async_computation | async-start | bytes 524288 | tf_op jit(solution)/shard_map/all_to_all | solution.py:264
  12.3 0.0 copy-start.10
  12.3 0.6 copy-done.9
  12.9 0.0 copy-done.10
  12.9 0.8 copy-done.6
  13.7 0.7 copy-done.7
  14.4 1.1 %intra.1 = (f32[512,512]{1,0:T(8,128)S(1)}, s32[8,128]{1,0:T(8,128)S(1)}, f32[4,16,128]{2,1,0:T(8,128)S(1)}, f32[1,512]{1,0:T(1,128)S(1)}) custom-call(s32[8,128]{1,0:T(8,128)S(1)} %copy-done.9, s32[8,512]{1,0:T(8,128)S(1)} %copy-done.7, f32[4,16,128]{2,1,0:T(8,128)S(1)} %copy-done.6, bf16[512,512]{1,0:T(8,128)(2,1)S(1)} %copy-done.1, ...), custom_call_target="tpu_custom_call" | custom-call | flops 536870912 | bytes 2715648 | tf_op jit(solution)/shard_map/intra/pallas_call | solution.py:232
  15.5 6.6 %all-to-all-done.x_ref = f32[16,32,128]{2,1,0:T(8,128)S(1)} async-done(((f32[16,32,128]{2,1,0:T(8,128)}), f32[16,32,128]{2,1,0:T(8,128)S(1)}, u32[]{:S(2)}, u32[]{:S(2)}) %all-to-all-start) | async-done | bytes 262176 | tf_op jit(solution)/shard_map/all_to_all | solution.py:264
  22.2 14.3 %all_to_all.25 = f32[16,32,128]{2,1,0:T(8,128)S(1)} all-to-all(f32[16,32,128]{2,1,0:T(8,128)S(1)} %state_scan.2), channel_id=1, replica_groups={{0,8,16,24,32,40,48,56,64,72,80,88,96,104,112,120},{65,121,73,113,81,10..., dimensions={0} | all-to-all | bytes 524288 | tf_op jit(solution)/shard_map/all_to_all | solution.py:264
  36.5 0.0 copy-done
  36.5 0.6 attend.1
  37.0 9.5 %all_to_all.26.sums_ref = f32[8,8,128]{2,1,0:T(8,128)S(1)} all-to-all(f32[8,8,128]{2,1,0:T(8,128)S(1)} %get-tuple-element.29), channel_id=1, replica_groups=mesh['seq'=64,'head'=8] {'head'}, dimensions={0} | all-to-all | bytes 65536 | tf_op jit(solution)/shard_map/all_to_all | solution.py:300
  46.6 0.6 normed_grad.1
  47.2 0.0 copy-start.4
  47.2 13.6 %all_to_all.27.x_ref = f32[16,32,128]{2,1,0:T(8,128)S(1)} all-to-all(f32[16,32,128]{2,1,0:T(8,128)S(1)} %bitcast.8), channel_id=1, replica_groups={{0,8,16,24,32,40,48,56,64,72,80,88,96,104,112,120},{1,57,9,49,17,41,25,..., dimensions={0} | all-to-all | bytes 524288 | tf_op jit(solution)/shard_map/all_to_all | solution.py:264
  60.8 0.7 state_scan.3
  61.6 4.7 %all-to-all-start.4 = ((f32[16,32,128]{2,1,0:T(8,128)}), f32[16,32,128]{2,1,0:T(8,128)S(1)}, u32[]{:S(2)}, u32[]{:S(2)}) async-start(f32[16,32,128]{2,1,0:T(8,128)} %state_scan.3), calls=%async_computation.4 | async-start | bytes 524288 | tf_op jit(solution)/shard_map/all_to_all | solution.py:264
  66.3 0.0 copy-start.5
  66.3 1.0 %copy-done.5 = bf16[512,512]{1,0:T(8,128)(2,1)S(1)} copy-done((bf16[512,512]{1,0:T(8,128)(2,1)S(1)}, bf16[512,512]{1,0:T(8,128)(2,1)}, u32[]{:S(2)}) %copy-start.5) | copy-done | bytes 524312
  67.3 3.3 %products.1 = (bf16[512,512]{1,0:T(8,128)(2,1)}, bf16[512,512]{1,0:T(8,128)(2,1)S(1)}, bf16[512,512]{1,0:T(8,128)(2,1)S(1)}) custom-call(s32[8,128]{1,0:T(8,128)S(1)} %get-tuple-element.23.bounds_ref, s32[8,512]{1,0:T(8,128)S(1)} %copy-done.8, bf16[512,512]{1,0:T(8,128)(2,1)S(1)} %copy-done.1, bf16[512,512]{1,0:T(8,128)(2,1)S(1)} %copy-done.2, ...), custom_call_target="tpu_custom_call" | custom-call | flops 1409286144 | bytes 3952640 | tf_op jit(solution)/shard_map/products/pallas_call | solution.py:232
  70.7 5.3 %all-to-all-done.4 = f32[16,32,128]{2,1,0:T(8,128)S(1)} async-done(((f32[16,32,128]{2,1,0:T(8,128)}), f32[16,32,128]{2,1,0:T(8,128)S(1)}, u32[]{:S(2)}, u32[]{:S(2)}) %all-to-all-start.4) | async-done | bytes 262176 | tf_op jit(solution)/shard_map/all_to_all | solution.py:264
  76.0 1.3 %key_value_grad.1 = (bf16[512,512]{1,0:T(8,128)(2,1)}, bf16[512,512]{1,0:T(8,128)(2,1)}) custom-call(s32[8,128]{1,0:T(8,128)S(1)} %get-tuple-element.23.bounds_ref, bf16[512,512]{1,0:T(8,128)(2,1)S(1)} %copy-done.2, bf16[512,512]{1,0:T(8,128)(2,1)S(1)} %copy-done.3, bf16[512,512]{1,0:T(8,128)(2,1)S(1)} %get-tuple-element.32.dk_ref, ...), custom_call_target="tpu_custom_call" | custom-call | flops 134217728 | bytes 3411968 | tf_op jit(solution)/shard_map/key_value_grad/pallas_call | solution.py:232
  (13 shorter events, 0.1 us)
Async XLA Ops:
  0.6 11.6 %copy-start.2 = (bf16[512,512]{1,0:T(8,128)(2,1)S(1)}, bf16[512,512]{1,0:T(8,128)(2,1)}, u32[]{:S(2)}) copy-start(bf16[512,512]{1,0:T(8,128)(2,1)} %k_ref.5) | copy-start | bytes 1572868
  0.6 11.6 %copy-start.3 = (bf16[512,512]{1,0:T(8,128)(2,1)S(1)}, bf16[512,512]{1,0:T(8,128)(2,1)}, u32[]{:S(2)}) copy-start(bf16[512,512]{1,0:T(8,128)(2,1)} %v_ref.5) | copy-start | bytes 1572868
  3.1 9.2 %copy-start.1 = (bf16[512,512]{1,0:T(8,128)(2,1)S(1)}, bf16[512,512]{1,0:T(8,128)(2,1)}, u32[]{:S(2)}) copy-start(bf16[512,512]{1,0:T(8,128)(2,1)} %q_ref.7) | copy-start | bytes 1572868
  3.1 19.1 %all-to-all-start = ((f32[16,32,128]{2,1,0:T(8,128)}), f32[16,32,128]{2,1,0:T(8,128)S(1)}, u32[]{:S(2)}, u32[]{:S(2)}) async-start(f32[16,32,128]{2,1,0:T(8,128)} %bitcast.10), calls=%async_computation | async-start | bytes 524288 | tf_op jit(solution)/shard_map/all_to_all | solution.py:264
  12.2 0.7 copy-start.9
  12.3 0.7 copy-start.10
  12.9 0.8 copy-start.6
  13.7 0.7 copy-start.7
  22.1 14.3 %copy-start = (bf16[512,512]{1,0:T(8,128)(2,1)S(1)}, bf16[512,512]{1,0:T(8,128)(2,1)}, u32[]{:S(2)}) copy-start(bf16[512,512]{1,0:T(8,128)(2,1)} %g_ref.3) | copy-start | bytes 1572868
  47.2 13.6 %copy-start.4 = (bf16[512,512]{1,0:T(8,128)(2,1)}, bf16[512,512]{1,0:T(8,128)(2,1)S(1)}, u32[]{:S(2)}) copy-start(bf16[512,512]{1,0:T(8,128)(2,1)S(1)} %get-tuple-element.30.normed_ref) | copy-start | bytes 1572868
  61.6 4.7 %copy-start.8 = (s32[8,512]{1,0:T(8,128)S(1)}, s32[8,512]{1,0:T(8,128)}, u32[]{:S(2)}) copy-start(s32[8,512]{1,0:T(8,128)} %get-tuple-element.21.edges_ref) | copy-start | bytes 49156
  61.6 14.4 %all-to-all-start.4 = ((f32[16,32,128]{2,1,0:T(8,128)}), f32[16,32,128]{2,1,0:T(8,128)S(1)}, u32[]{:S(2)}, u32[]{:S(2)}) async-start(f32[16,32,128]{2,1,0:T(8,128)} %state_scan.3), calls=%async_computation.4 | async-start | bytes 524288 | tf_op jit(solution)/shard_map/all_to_all | solution.py:264
  66.3 1.0 %copy-start.5 = (bf16[512,512]{1,0:T(8,128)(2,1)S(1)}, bf16[512,512]{1,0:T(8,128)(2,1)}, u32[]{:S(2)}) copy-start(bf16[512,512]{1,0:T(8,128)(2,1)} %copy-done.4) | copy-start | bytes 1572868

commit v5 on v4

--- a/solution.py
+++ b/solution.py
@@ -11,7 +11,7 @@
 WIDTH = 4096
 EPSILON = 1e-06
 QUARTERS = 4
-LOADS = 4
+LOADS = 1
 
 F32 = jnp.float32
 BF16 = jnp.bfloat16

time: 77.9 us -> 77.9 us (level)
  no operation moved by 1% of the time
where the time goes in v5:
time: 77.9 us; the launch traced here: 77.2 us
  blocking collectives  37.4 us (48%)
  starting transfers between devices  13.8 us (18%)
  waiting for transfers between devices  11.9 us (15%)
  Pallas kernels  10.1 us (13%)
  local copies, waits for them, and re-layouts  3.19 us (4%)
    all_to_all x2, blocking collectives, swap(): lax.all_to_all(x.reshape(pieces), ('seq', 'head'), 0, 0, axis_index_group...  27.9 us
    all_to_all x2, starting transfers between devices, swap(): lax.all_to_all(x.reshape(pieces), ('seq', 'head'), 0, 0, axis_index_group...  13.8 us
    all_to_all x2, waiting for transfers between devices, swap(): lax.all_to_all(x.reshape(pieces), ('seq', 'head'), 0, 0, axis_index_group...  11.9 us
    pallas_call x8, Pallas kernels, call(): pl.pallas_call(kernel, out_shape=out_shape, in_specs=in_specs or [VMEM] *...  10.1 us
    all_to_all x1, blocking collectives, on_device(): sums = lax.all_to_all(sums, 'head', 0, 0, tiled=True)  9.52 us
    unnamed x22, local copies, waits for them, and re-layouts  3.19 us
  transfers between devices with their start and end apart: 2, of which 2 were waited for; matrix products, arithmetic and copies ran while one was open for 0% of the time, Pallas kernels for 6%

profile of v5, /device:TPU:128, one launch (start us, length us, event | category | flops | bytes accessed | tf_op | source)
XLA Modules:
  0.0 77.2 jit_solution(16110650876907903938)
XLA Ops:
  0.6 0.0 copy-start.2
  0.7 2.4 %kv_state.1 = (f32[4,128,128]{2,1,0:T(8,128)}, s32[8,128]{1,0:T(8,128)}, s32[8,512]{1,0:T(8,128)}, f32[4,16,128]{2,1,0:T(8,128)}) custom-call(s32[25]{0:T(128)} %starts_hbm.1, bf16[512,512]{1,0:T(8,128)(2,1)} %k_ref.5, bf16[512,512]{1,0:T(8,128)(2,1)} %v_ref.5), custom_call_target="tpu_custom_call" | custom-call | flops 67108864 | bytes 1364068 | tf_op jit(solution)/shard_map/kv_state/pallas_call | solution.py:232
  3.0 0.0 copy-start.1
  3.1 9.2 %all-to-all-start = ((f32[16,32,128]{2,1,0:T(8,128)}), f32[16,32,128]{2,1,0:T(8,128)S(1)}, u32[]{:S(2)}, u32[]{:S(2)}) async-start(f32[16,32,128]{2,1,0:T(8,128)} %bitcast.10), calls=%async_computation | async-start | bytes 524288 | tf_op jit(solution)/shard_map/all_to_all | solution.py:264
  12.2 0.0 copy-start.10
  12.3 0.6 copy-done.9
  12.9 0.0 copy-done.10
  12.9 0.8 copy-done.6
  13.7 0.7 copy-done.7
  14.4 1.1 %intra.1 = (f32[512,512]{1,0:T(8,128)S(1)}, s32[8,128]{1,0:T(8,128)S(1)}, f32[4,16,128]{2,1,0:T(8,128)S(1)}, f32[1,512]{1,0:T(1,128)S(1)}) custom-call(s32[8,128]{1,0:T(8,128)S(1)} %copy-done.9, s32[8,512]{1,0:T(8,128)S(1)} %copy-done.7, f32[4,16,128]{2,1,0:T(8,128)S(1)} %copy-done.6, bf16[512,512]{1,0:T(8,128)(2,1)S(1)} %copy-done.1, ...), custom_call_target="tpu_custom_call" | custom-call | flops 536870912 | bytes 2715648 | tf_op jit(solution)/shard_map/intra/pallas_call | solution.py:232
  15.5 6.6 %all-to-all-done.x_ref = f32[16,32,128]{2,1,0:T(8,128)S(1)} async-done(((f32[16,32,128]{2,1,0:T(8,128)}), f32[16,32,128]{2,1,0:T(8,128)S(1)}, u32[]{:S(2)}, u32[]{:S(2)}) %all-to-all-start) | async-done | bytes 262176 | tf_op jit(solution)/shard_map/all_to_all | solution.py:264
  22.2 14.3 %all_to_all.25 = f32[16,32,128]{2,1,0:T(8,128)S(1)} all-to-all(f32[16,32,128]{2,1,0:T(8,128)S(1)} %state_scan.2), channel_id=1, replica_groups={{0,8,16,24,32,40,48,56,64,72,80,88,96,104,112,120},{65,121,73,113,81,10..., dimensions={0} | all-to-all | bytes 524288 | tf_op jit(solution)/shard_map/all_to_all | solution.py:264
  36.5 0.6 attend.1
  37.0 9.5 %all_to_all.26.sums_ref = f32[8,8,128]{2,1,0:T(8,128)S(1)} all-to-all(f32[8,8,128]{2,1,0:T(8,128)S(1)} %get-tuple-element.29), channel_id=1, replica_groups=mesh['seq'=64,'head'=8] {'head'}, dimensions={0} | all-to-all | bytes 65536 | tf_op jit(solution)/shard_map/all_to_all | solution.py:300
  46.5 0.6 normed_grad.1
  47.2 0.0 copy-start.4
  47.2 13.6 %all_to_all.27.x_ref = f32[16,32,128]{2,1,0:T(8,128)S(1)} all-to-all(f32[16,32,128]{2,1,0:T(8,128)S(1)} %bitcast.8), channel_id=1, replica_groups={{0,8,16,24,32,40,48,56,64,72,80,88,96,104,112,120},{1,57,9,49,17,41,25,..., dimensions={0} | all-to-all | bytes 524288 | tf_op jit(solution)/shard_map/all_to_all | solution.py:264
  60.8 0.7 state_scan.3
  61.5 4.7 %all-to-all-start.4 = ((f32[16,32,128]{2,1,0:T(8,128)}), f32[16,32,128]{2,1,0:T(8,128)S(1)}, u32[]{:S(2)}, u32[]{:S(2)}) async-start(f32[16,32,128]{2,1,0:T(8,128)} %state_scan.3), calls=%async_computation.4 | async-start | bytes 524288 | tf_op jit(solution)/shard_map/all_to_all | solution.py:264
  66.2 0.0 copy-start.5
  66.2 1.0 %copy-done.5 = bf16[512,512]{1,0:T(8,128)(2,1)S(1)} copy-done((bf16[512,512]{1,0:T(8,128)(2,1)S(1)}, bf16[512,512]{1,0:T(8,128)(2,1)}, u32[]{:S(2)}) %copy-start.5) | copy-done | bytes 524312
  67.3 3.3 %products.1 = (bf16[512,512]{1,0:T(8,128)(2,1)}, bf16[512,512]{1,0:T(8,128)(2,1)S(1)}, bf16[512,512]{1,0:T(8,128)(2,1)S(1)}) custom-call(s32[8,128]{1,0:T(8,128)S(1)} %get-tuple-element.23.bounds_ref, s32[8,512]{1,0:T(8,128)S(1)} %copy-done.8, bf16[512,512]{1,0:T(8,128)(2,1)S(1)} %copy-done.1, bf16[512,512]{1,0:T(8,128)(2,1)S(1)} %copy-done.2, ...), custom_call_target="tpu_custom_call" | custom-call | flops 1409286144 | bytes 3952640 | tf_op jit(solution)/shard_map/products/pallas_call | solution.py:232
  70.6 5.3 %all-to-all-done.4 = f32[16,32,128]{2,1,0:T(8,128)S(1)} async-done(((f32[16,32,128]{2,1,0:T(8,128)}), f32[16,32,128]{2,1,0:T(8,128)S(1)}, u32[]{:S(2)}, u32[]{:S(2)}) %all-to-all-start.4) | async-done | bytes 262176 | tf_op jit(solution)/shard_map/all_to_all | solution.py:264
  75.9 1.3 %key_value_grad.1 = (bf16[512,512]{1,0:T(8,128)(2,1)}, bf16[512,512]{1,0:T(8,128)(2,1)}) custom-call(s32[8,128]{1,0:T(8,128)S(1)} %get-tuple-element.23.bounds_ref, bf16[512,512]{1,0:T(8,128)(2,1)S(1)} %copy-done.2, bf16[512,512]{1,0:T(8,128)(2,1)S(1)} %copy-done.3, bf16[512,512]{1,0:T(8,128)(2,1)S(1)} %get-tuple-element.32.dk_ref, ...), custom_call_target="tpu_custom_call" | custom-call | flops 134217728 | bytes 3411968 | tf_op jit(solution)/shard_map/key_value_grad/pallas_call | solution.py:232
  (13 shorter events, 0.1 us)
Async XLA Ops:
  0.6 11.6 %copy-start.2 = (bf16[512,512]{1,0:T(8,128)(2,1)S(1)}, bf16[512,512]{1,0:T(8,128)(2,1)}, u32[]{:S(2)}) copy-start(bf16[512,512]{1,0:T(8,128)(2,1)} %k_ref.5) | copy-start | bytes 1572868
  0.6 11.6 %copy-start.3 = (bf16[512,512]{1,0:T(8,128)(2,1)S(1)}, bf16[512,512]{1,0:T(8,128)(2,1)}, u32[]{:S(2)}) copy-start(bf16[512,512]{1,0:T(8,128)(2,1)} %v_ref.5) | copy-start | bytes 1572868
  3.0 9.2 %copy-start.1 = (bf16[512,512]{1,0:T(8,128)(2,1)S(1)}, bf16[512,512]{1,0:T(8,128)(2,1)}, u32[]{:S(2)}) copy-start(bf16[512,512]{1,0:T(8,128)(2,1)} %q_ref.7) | copy-start | bytes 1572868
  3.1 19.1 %all-to-all-start = ((f32[16,32,128]{2,1,0:T(8,128)}), f32[16,32,128]{2,1,0:T(8,128)S(1)}, u32[]{:S(2)}, u32[]{:S(2)}) async-start(f32[16,32,128]{2,1,0:T(8,128)} %bitcast.10), calls=%async_computation | async-start | bytes 524288 | tf_op jit(solution)/shard_map/all_to_all | solution.py:264
  12.2 0.7 copy-start.9
  12.2 0.7 copy-start.10
  12.9 0.8 copy-start.6
  13.7 0.7 copy-start.7
  22.1 14.3 %copy-start = (bf16[512,512]{1,0:T(8,128)(2,1)S(1)}, bf16[512,512]{1,0:T(8,128)(2,1)}, u32[]{:S(2)}) copy-start(bf16[512,512]{1,0:T(8,128)(2,1)} %g_ref.3) | copy-start | bytes 1572868
  47.2 13.6 %copy-start.4 = (bf16[512,512]{1,0:T(8,128)(2,1)}, bf16[512,512]{1,0:T(8,128)(2,1)S(1)}, u32[]{:S(2)}) copy-start(bf16[512,512]{1,0:T(8,128)(2,1)S(1)} %get-tuple-element.30.normed_ref) | copy-start | bytes 1572868
  61.5 4.7 %copy-start.8 = (s32[8,512]{1,0:T(8,128)S(1)}, s32[8,512]{1,0:T(8,128)}, u32[]{:S(2)}) copy-start(s32[8,512]{1,0:T(8,128)} %get-tuple-element.21.edges_ref) | copy-start | bytes 49156
  61.5 14.4 %all-to-all-start.4 = ((f32[16,32,128]{2,1,0:T(8,128)}), f32[16,32,128]{2,1,0:T(8,128)S(1)}, u32[]{:S(2)}, u32[]{:S(2)}) async-start(f32[16,32,128]{2,1,0:T(8,128)} %state_scan.3), calls=%async_computation.4 | async-start | bytes 524288 | tf_op jit(solution)/shard_map/all_to_all | solution.py:264
  66.2 1.0 %copy-start.5 = (bf16[512,512]{1,0:T(8,128)(2,1)S(1)}, bf16[512,512]{1,0:T(8,128)(2,1)}, u32[]{:S(2)}) copy-start(bf16[512,512]{1,0:T(8,128)(2,1)} %copy-done.4) | copy-start | bytes 1572868
